TPU v7x, 512 devices: a whole 4x8x8 slice. The times are simulated.
512 devices in a mesh: gx: 8 (over y), gy: 8 (over z_hi, core), gz: 8 (over x, z_lo).
Axes of the slice: x: 4, y: 8, z: 8 (z_hi: 4, z_lo: 2; z = z_hi * 2 + z_lo), core: 2. Of those that a mesh axis runs over, the one named last changes fastest.
Arguments:
- volume: bfloat16 [64, 256, 128, 32], P('gx', 'gy', 'gz'), may hold values from -6 to 6
- conv_in: bfloat16 [3, 3, 3, 32, 32], replicated, may hold values from -0.21875 to 0.21875
- conv_out: bfloat16 [3, 3, 3, 32, 32], replicated, may hold values from -0.21875 to 0.21875
- norm_gain: float32 [256], replicated, may hold values from 0.1 to 1.9
- q_weight: bfloat16 [256, 256], replicated, may hold values from -3 to 3
- kv_weight: bfloat16 [256, 512], replicated, may hold values from -0.375 to 0.375
- out_weight: bfloat16 [256, 256], replicated, may hold values from -0.375 to 0.375
- up_weight: bfloat16 [256, 256], replicated, may hold values from -0.375 to 0.375
Outputs:
- joined_out: bfloat16 [64, 256, 128, 32], P('gx', 'gy', 'gz')
All inputs are finite; a program needn't handle non-finite values.
Results may differ from a plain program's by a relative error of at most 0.012.
The roundings to bfloat16 on the way count: a program that leaves them out, or rounds other values in their place, can miss the bound.
Values may be sent and summed in bfloat16 or wider, within the bound.
A program may use at most 64 MiB of HBM per device.

v0:
```python
import math

import jax
import jax.numpy as jnp
from jax import lax
from jax.sharding import PartitionSpec as P

HEADS = 8


def from_behind(array, axis, by):
    devices = lax.axis_size(axis)
    pairs = [(i, i + by) for i in range(devices) if 0 <= i + by < devices]
    return lax.ppermute(array, axis, pairs)


def joined_along(parts, dim):
    shape = list(parts.shape[1:])
    shape[dim] *= parts.shape[0]
    return jnp.moveaxis(parts, 0, dim).reshape(shape)


def copy_for_each(array, axis):
    devices = lax.axis_size(axis)
    return lax.all_to_all(
        jnp.broadcast_to(array[None], (devices, *array.shape)), axis, 0, 0, tiled=True
    )


def collect(array, axis, dim):
    return joined_along(copy_for_each(array, axis), dim)


def convolve(padded, kernel):
    return lax.conv_general_dilated(
        padded[None],
        kernel,
        (1, 1, 1),
        "VALID",
        dimension_numbers=("NDHWC", "DHWIO", "NDHWC"),
        preferred_element_type=jnp.float32,
    )[0]


def pad_brick(brick):
    lower_rim = from_behind(brick[:, :, -1:], "gz", 1)
    upper_rim = from_behind(brick[:, :, :1], "gz", -1)
    widened = jnp.concatenate([lower_rim, brick, upper_rim], axis=2)
    lower_rim = from_behind(widened[:, -1:], "gy", 1)
    upper_rim = from_behind(widened[:, :1], "gy", -1)
    widened = jnp.concatenate([lower_rim, widened, upper_rim], axis=1)
    lower_rim = from_behind(widened[-1:], "gx", 1)
    upper_rim = from_behind(widened[:1], "gx", -1)
    return jnp.concatenate([lower_rim, widened, upper_rim], axis=0)


def tokenize(volume_map):
    extent_x, extent_y, extent_z, channels = volume_map.shape
    grid_cells = volume_map.reshape(
        extent_x // 8, 2, 4, extent_y // 8, 2, 4, extent_z // 8, 2, 4, channels
    ).mean(axis=(2, 5, 8))
    grid_cells = grid_cells.transpose(0, 2, 4, 1, 3, 5, 6)
    return grid_cells.reshape(extent_x // 8 * (extent_y // 8) * (extent_z // 8), 8 * channels)


def spread_cells(token_rows, extent_x, extent_y, extent_z):
    channels = token_rows.shape[1] // 8
    grid_cells = token_rows.reshape(
        extent_x // 8, extent_y // 8, extent_z // 8, 2, 2, 2, channels
    ).transpose(0, 3, 1, 4, 2, 5, 6)
    grid_cells = jnp.broadcast_to(
        grid_cells[:, :, None, :, :, None, :, :, None, :],
        (extent_x // 8, 2, 4, extent_y // 8, 2, 4, extent_z // 8, 2, 4, channels),
    )
    return grid_cells.reshape(extent_x, extent_y, extent_z, channels)


def layer_norm(tokens, norm_gain):
    center = tokens - tokens.mean(axis=1, keepdims=True)
    spread = (center * center).mean(axis=1, keepdims=True)
    return (center * lax.rsqrt(spread + 1e-05) * norm_gain).astype(jnp.bfloat16)


def make_folder(queries, running, shard_piece):
    scaling = queries.shape[-1] ** (-0.5)
    key_count = shard_piece.shape[2]
    block_rows = math.gcd(key_count, 1024)

    def advance(position, state):
        peak_score, denominator, numerator = state
        head_keys = lax.dynamic_slice_in_dim(shard_piece[0], position * block_rows, block_rows, 1)
        head_values = lax.dynamic_slice_in_dim(shard_piece[1], position * block_rows, block_rows, 1)
        scores = (
            jnp.einsum("hqd,hkd->hqk", queries, head_keys, preferred_element_type=jnp.float32)
            * scaling
        )
        new_peak = jnp.maximum(peak_score, scores.max(axis=-1))
        rescale = jnp.exp(peak_score - new_peak)
        weights = jnp.exp(scores - new_peak[..., None])
        denominator = denominator * rescale + weights.sum(axis=-1)
        numerator = numerator * rescale[..., None] + jnp.einsum(
            "hqk,hkd->hqd",
            weights.astype(jnp.bfloat16),
            head_values,
            preferred_element_type=jnp.float32,
        )
        return (new_peak, denominator, numerator)

    return lax.fori_loop(0, key_count // block_rows, advance, running)


def start_state(queries):
    heads_here, query_count, head_size = queries.shape
    return (
        jnp.full((heads_here, query_count), -1e30, jnp.float32),
        jnp.zeros((heads_here, query_count), jnp.float32),
        jnp.zeros((heads_here, query_count, head_size), jnp.float32),
    )


def finish(running):
    return (running[2] / running[1][..., None]).astype(jnp.bfloat16)


def on_device(volume, conv_in, conv_out, norm_gain, q_weight, kv_weight, out_weight, up_weight):
    extent_x, extent_y, extent_z, channels = volume.shape
    encoded = jax.nn.relu(convolve(pad_brick(volume), conv_in)).astype(jnp.bfloat16)
    tokens = tokenize(encoded.astype(jnp.float32))
    normed = layer_norm(tokens, norm_gain)
    queries = jnp.dot(normed, q_weight, preferred_element_type=jnp.float32).astype(jnp.bfloat16)
    key_value = jnp.dot(normed, kv_weight, preferred_element_type=jnp.float32).astype(jnp.bfloat16)
    token_count, width = tokens.shape
    head_size = width // HEADS
    packed = (
        jnp.concatenate([queries, key_value], axis=1)
        .reshape(token_count, 3, HEADS, head_size)
        .transpose(1, 2, 0, 3)
    )
    arranged = lax.all_to_all(packed, "gz", split_axis=1, concat_axis=2, tiled=True)
    head_queries = arranged[0]
    running = make_folder(
        head_queries, start_state(head_queries), collect(arranged[1:], ("gx", "gy"), 2)
    )
    returned = lax.all_to_all(finish(running), "gz", split_axis=1, concat_axis=0, tiled=True)
    attended = returned.transpose(1, 0, 2).reshape(token_count, width)
    mixture = (tokens + jnp.dot(attended, out_weight, preferred_element_type=jnp.float32)).astype(
        jnp.bfloat16
    )
    upward = jnp.dot(mixture, up_weight, preferred_element_type=jnp.float32)
    joined = (
        encoded.astype(jnp.float32) + spread_cells(upward, extent_x, extent_y, extent_z)
    ).astype(jnp.bfloat16)
    return convolve(pad_brick(joined), conv_out).astype(jnp.bfloat16)


def solution(mesh):
    placed = (P("gx", "gy", "gz", None), P(), P(), P(), P(), P(), P(), P())
    return jax.shard_map(
        on_device, mesh=mesh, in_specs=placed, out_specs=P("gx", "gy", "gz", None), check_vma=False
    )
```

profile of v0, /device:TPU:1, one launch (start us, length us, event | category | flops | bytes accessed | tf_op | source)
XLA Modules:
  0.0 177.9 jit_solution(2297564431249466196)
XLA Ops:
  0.0 2.0 %copy.103 = bf16[8,32,16,32]{1,3,2,0:T(8,128)(2,1)S(1)} copy(bf16[8,32,16,32]{3,2,1,0:T(8,128)(2,1)} %param.10) | data formatting | bytes 524288 | tf_op args[0]
  2.0 4.8 %collective-permute-start = (bf16[8,32,1,32]{1,3,2,0:T(8,128)(2,1)S(1)}, bf16[8,32,1,32]{1,3,2,0:T(8,128)(2,1)S(1)}, u32[]{:S(2)}, u32[]{:S(2)}) collective-permute-start(bf16[8,32,1,32]{1,3,2,0:T(8,128)(2,1)S(1)} %get-tuple-element.184), channel_id=1, source_target_pairs={{0,1},{1,2},{2,3},{3,4},{4,5},{5,6},{6,7},{8,9},{9,10},{10,11},{11... | collective-permute-start | bytes 49160 | tf_op jit(solution)/shard_map/ppermute | solution.py:14
  6.8 1.3 collective-permute-start.1
  8.2 3.7 %collective-permute-done.1 = bf16[8,32,1,32]{1,3,2,0:T(8,128)(2,1)S(1)} collective-permute-done((bf16[8,32,1,32]{1,3,2,0:T(8,128)(2,1)S(1)}, bf16[8,32,1,32]{1,3,2,0:T(8,128)(2,1)S(1)}, u32[]{:S(2)}, u32[]{:S(2)}) %collective-permute-start.1) | collective-permute-done | bytes 16416 | tf_op jit(solution)/shard_map/ppermute | solution.py:14
  12.1 1.6 fusion.49
  13.7 2.2 %copy.106 = bf16[8,1,18,32]{3,0,2,1:T(8,128)(2,1)S(1)} copy(bf16[8,1,18,32]{1,3,2,0:T(8,128)(2,1)} %get-tuple-element.180) | data formatting | bytes 18432 | tf_op jit(solution)/shard_map/slice | solution.py:49
  15.9 7.8 %collective-permute-start.2 = (bf16[8,1,18,32]{3,0,2,1:T(8,128)(2,1)S(1)}, bf16[8,1,18,32]{3,0,2,1:T(8,128)(2,1)S(1)}, u32[]{:S(2)}, u32[]{:S(2)}) collective-permute-start(bf16[8,1,18,32]{3,0,2,1:T(8,128)(2,1)S(1)} %copy.106), channel_id=1, source_target_pairs={{0,8},{8,16},{16,24},{24,32},{32,40},{40,48},{48,56},{1,9},{9,17},... | collective-permute-start | bytes 27656 | tf_op jit(solution)/shard_map/ppermute | solution.py:14
  24.6 1.9 %collective-permute-start.3 = (bf16[8,1,18,32]{3,0,2,1:T(8,128)(2,1)S(1)}, bf16[8,1,18,32]{3,0,2,1:T(8,128)(2,1)S(1)}, u32[]{:S(2)}, u32[]{:S(2)}) collective-permute-start(bf16[8,1,18,32]{3,0,2,1:T(8,128)(2,1)S(1)} %copy.107), channel_id=1, source_target_pairs={{8,0},{16,8},{24,16},{32,24},{40,32},{48,40},{56,48},{9,1},{17,9},... | collective-permute-start | bytes 27656 | tf_op jit(solution)/shard_map/ppermute | solution.py:14
  27.5 3.3 %collective-permute-done.3 = bf16[8,1,18,32]{3,0,2,1:T(8,128)(2,1)S(1)} collective-permute-done((bf16[8,1,18,32]{3,0,2,1:T(8,128)(2,1)S(1)}, bf16[8,1,18,32]{3,0,2,1:T(8,128)(2,1)S(1)}, u32[]{:S(2)}, u32[]{:S(2)}) %collective-permute-start.3) | collective-permute-done | bytes 9248 | tf_op jit(solution)/shard_map/ppermute | solution.py:14
  30.8 2.0 %copy.109 = bf16[8,1,18,32]{1,3,2,0:T(8,128)(2,1)} copy(bf16[8,1,18,32]{3,0,2,1:T(8,128)(2,1)S(1)} %collective-permute-done.3) | data formatting | bytes 18432 | tf_op jit(solution)/shard_map/ppermute | solution.py:14
  32.8 1.4 pad_maximum_fusion.10
  34.1 3.2 %collective-permute-start.4 = (bf16[1,34,18,32]{1,3,2,0:T(8,128)(2,1)S(1)}, bf16[1,34,18,32]{1,3,2,0:T(8,128)(2,1)S(1)}, u32[]{:S(2)}, u32[]{:S(2)}) collective-permute-start(bf16[1,34,18,32]{1,3,2,0:T(8,128)(2,1)S(1)} %get-tuple-element.174), channel_id=1, source_target_pairs={{0,64},{64,128},{128,192},{192,256},{256,320},{320,384},{384,448},... | collective-permute-start | bytes 117512 | tf_op jit(solution)/shard_map/ppermute | solution.py:14
  37.3 1.5 collective-permute-start.5
  39.4 3.8 %collective-permute-done.5 = bf16[1,34,18,32]{1,3,2,0:T(8,128)(2,1)S(1)} collective-permute-done((bf16[1,34,18,32]{1,3,2,0:T(8,128)(2,1)S(1)}, bf16[1,34,18,32]{1,3,2,0:T(8,128)(2,1)S(1)}, u32[]{:S(2)}, u32[]{:S(2)}) %collective-permute-start.5) | collective-permute-done | bytes 39200 | tf_op jit(solution)/shard_map/ppermute | solution.py:14
  43.2 1.1 maximum_bitcast_fusion.1
  44.8 3.1 %copy.111 = bf16[10,34,1,8,3,32]{5,3,4,1,0,2:T(8,128)(2,1)} copy(bf16[10,34,1,8,3,32]{1,5,4,3,2,0:T(8,128)(2,1)S(1)} %bitcast.117) | data formatting | bytes 1044480 | tf_op jit(solution)/shard_map/conv_general_dilated | solution.py:35
  47.9 1.9 %slice.83 = bf16[10,34,1,7,2,32]{5,3,4,1,0,2:T(8,128)(2,1)S(1)} slice(bf16[10,34,1,8,3,32]{5,3,4,1,0,2:T(8,128)(2,1)} %copy.111), slice={[0:10], [0:34], [0:1], [1:8], [0:2], [0:32]} | slice | bytes 609280 | tf_op jit(solution)/shard_map/conv_general_dilated | solution.py:35
  49.9 4.4 %maximum_convert_fusion = bf16[8,32,8,3,32]{4,2,3,1,0:T(8,128)(2,1)S(1)} fusion(pred[8,3]{0,1:T(4,128)(4,1)S(1)} %copy-done.12, bf16[3,3,3,32,32]{4,3,2,1,0:T(8,128)(2,1)S(1)} %copy-done.8, bf16[10,34,1,7,2,32]{5,3,4,1,0,2:T(8,128)(2,1)S(1)} %slice.83, bf16[10,34,1,8,3,32]{5,3,4,1,0,2:T(8,128)(2,1)S(1)} %copy-done.5), kind=kOutput, calls=%fused_computation.38 | convolution fusion | flops 342939648 | bytes 1275416 | tf_op jit(solution)/shard_map/conv_general_dilated | solution.py:35
  54.6 1.2 copy-done.2
  58.1 9.5 %all_to_all.26 = bf16[8,2,384]{2,1,0:T(2,128)(2,1)S(1)} all-to-all(bf16[8,2,384]{2,1,0:T(2,128)(2,1)S(1)} %reshape.199), channel_id=1, replica_groups=mesh['gx'=8,'gy'=8,'gz'=8] {'gz'}, dimensions={0} | all-to-all | bytes 24576 | tf_op jit(solution)/shard_map/all_to_all | solution.py:139
  68.1 1.5 reshape.201
  69.6 18.1 %all-to-all-start.1 = ((bf16[64,2,2048]{2,1,0:T(2,128)(2,1)}), bf16[64,2,2048]{2,1,0:T(2,128)(2,1)S(1)}, u32[]{:S(2)}, u32[]{:S(2)}) async-start(bf16[64,2,2048]{2,1,0:T(2,128)(2,1)} %reshape.201), calls=%async_computation.1 | async-start | bytes 1048576 | tf_op jit(solution)/shard_map/all_to_all | solution.py:25
  87.8 19.5 %all-to-all-done.1 = bf16[64,2,2048]{2,1,0:T(2,128)(2,1)S(1)} async-done(((bf16[64,2,2048]{2,1,0:T(2,128)(2,1)}), bf16[64,2,2048]{2,1,0:T(2,128)(2,1)S(1)}, u32[]{:S(2)}, u32[]{:S(2)}) %all-to-all-start.1) | async-done | bytes 524320 | tf_op jit(solution)/shard_map/all_to_all | solution.py:25
  109.1 11.6 %while.18 = (s32[]{:T(128)}, f32[1,64]{1,0:T(1,128)S(1)}, f32[1,64]{1,0:T(1,128)S(1)}, f32[1,64,32]{1,2,0:T(8,128)S(1)}, bf16[2,1,4096,32]{3,2,1,0:T(8,128)(2,1)...) while((s32[]{:T(128)}, f32[1,64]{1,0:T(1,128)S(1)}, ...), condition=%wide.region_6.7_spmd.clone, body=%wide.region_3.6_spmd.clone.sunk | while | flops 8788359 | bytes 2396327 | solution.py:109
  109.1 1.1 fusion.71
  110.6 1.2 fusion.76
  112.0 1.1 fusion.71
  113.5 1.2 fusion.76
  116.4 1.2 fusion.76
  119.3 1.2 fusion.76
  122.2 7.4 %all_to_all.27 = bf16[8,2,128]{2,1,0:T(2,128)(2,1)S(1)} all-to-all(bf16[8,2,128]{2,1,0:T(2,128)(2,1)S(1)} %reshape.203), channel_id=1, replica_groups=mesh['gx'=8,'gy'=8,'gz'=8] {'gz'}, dimensions={0} | all-to-all | bytes 8192 | tf_op jit(solution)/shard_map/all_to_all | solution.py:144
  131.0 2.2 %collective-permute-start.6 = (bf16[8,32,1,32]{3,1,2,0:T(8,128)(2,1)S(1)}, bf16[8,32,1,32]{3,1,2,0:T(8,128)(2,1)S(1)}, u32[]{:S(2)}, u32[]{:S(2)}) collective-permute-start(bf16[8,32,1,32]{3,1,2,0:T(8,128)(2,1)S(1)} %get-tuple-element.182), channel_id=1, source_target_pairs={{0,1},{1,2},{2,3},{3,4},{4,5},{5,6},{6,7},{8,9},{9,10},{10,11},{11... | collective-permute-start | bytes 49160 | tf_op jit(solution)/shard_map/ppermute | solution.py:14
  133.2 1.3 collective-permute-start.7
  134.6 3.8 %collective-permute-done.7 = bf16[8,32,1,32]{3,1,2,0:T(8,128)(2,1)S(1)} collective-permute-done((bf16[8,32,1,32]{3,1,2,0:T(8,128)(2,1)S(1)}, bf16[8,32,1,32]{3,1,2,0:T(8,128)(2,1)S(1)}, u32[]{:S(2)}, u32[]{:S(2)}) %collective-permute-start.7) | collective-permute-done | bytes 16416 | tf_op jit(solution)/shard_map/ppermute | solution.py:14
  138.6 6.2 %collective-permute-start.8 = (bf16[8,1,18,32]{3,1,2,0:T(2,128)(2,1)S(1)}, bf16[8,1,18,32]{3,1,2,0:T(2,128)(2,1)S(1)}, u32[]{:S(2)}, u32[]{:S(2)}) collective-permute-start(bf16[8,1,18,32]{3,1,2,0:T(2,128)(2,1)S(1)} %get-tuple-element.178), channel_id=1, source_target_pairs={{0,8},{8,16},{16,24},{24,32},{32,40},{40,48},{48,56},{1,9},{9,17},... | collective-permute-start | bytes 27656 | tf_op jit(solution)/shard_map/ppermute | solution.py:14
  144.8 1.9 %collective-permute-start.9 = (bf16[8,1,18,32]{3,1,2,0:T(2,128)(2,1)S(1)}, bf16[8,1,18,32]{3,1,2,0:T(2,128)(2,1)S(1)}, u32[]{:S(2)}, u32[]{:S(2)}) collective-permute-start(bf16[8,1,18,32]{3,1,2,0:T(2,128)(2,1)S(1)} %get-tuple-element.179), channel_id=1, source_target_pairs={{8,0},{16,8},{24,16},{32,24},{40,32},{48,40},{56,48},{9,1},{17,9},... | collective-permute-start | bytes 27656 | tf_op jit(solution)/shard_map/ppermute | solution.py:14
  146.7 4.6 %collective-permute-done.9 = bf16[8,1,18,32]{3,1,2,0:T(2,128)(2,1)S(1)} collective-permute-done((bf16[8,1,18,32]{3,1,2,0:T(2,128)(2,1)S(1)}, bf16[8,1,18,32]{3,1,2,0:T(2,128)(2,1)S(1)}, u32[]{:S(2)}, u32[]{:S(2)}) %collective-permute-start.9) | collective-permute-done | bytes 9248 | tf_op jit(solution)/shard_map/ppermute | solution.py:14
  151.5 2.9 %collective-permute-start.10 = (bf16[1,34,18,32]{3,1,2,0:T(8,128)(2,1)S(1)}, bf16[1,34,18,32]{3,1,2,0:T(8,128)(2,1)S(1)}, u32[]{:S(2)}, u32[]{:S(2)}) collective-permute-start(bf16[1,34,18,32]{3,1,2,0:T(8,128)(2,1)S(1)} %get-tuple-element.176), channel_id=1, source_target_pairs={{0,64},{64,128},{128,192},{192,256},{256,320},{320,384},{384,448},... | collective-permute-start | bytes 117512 | tf_op jit(solution)/shard_map/ppermute | solution.py:14
  154.4 1.3 collective-permute-start.11
  155.7 1.2 collective-permute-done.10
  156.9 3.8 %collective-permute-done.11 = bf16[1,34,18,32]{3,1,2,0:T(8,128)(2,1)S(1)} collective-permute-done((bf16[1,34,18,32]{3,1,2,0:T(8,128)(2,1)S(1)}, bf16[1,34,18,32]{3,1,2,0:T(8,128)(2,1)S(1)}, u32[]{:S(2)}, u32[]{:S(2)}) %collective-permute-start.11) | collective-permute-done | bytes 39200 | tf_op jit(solution)/shard_map/ppermute | solution.py:14
  160.7 1.6 maximum_bitcast_fusion
  162.3 2.6 %copy.132 = bf16[10,34,1,18,32]{1,4,3,2,0:T(8,128)(2,1)} copy(bf16[10,34,1,18,32]{4,1,3,0,2:T(8,128)(2,1)S(1)} %maximum_bitcast_fusion) | data formatting | bytes 783360
  164.9 1.8 pad.2.clone
  166.6 3.1 %copy.126 = bf16[10,34,1,8,3,32]{5,3,4,1,0,2:T(8,128)(2,1)} copy(bf16[10,34,1,8,3,32]{1,5,4,3,2,0:T(8,128)(2,1)S(1)} %bitcast.116) | data formatting | bytes 1044480 | tf_op jit(solution)/shard_map/conv_general_dilated | solution.py:35
  169.7 1.9 %slice.89 = bf16[10,34,1,7,2,32]{5,3,4,1,0,2:T(8,128)(2,1)S(1)} slice(bf16[10,34,1,8,3,32]{5,3,4,1,0,2:T(8,128)(2,1)} %copy.126), slice={[0:10], [0:34], [0:1], [1:8], [0:2], [0:32]} | slice | bytes 609280 | tf_op jit(solution)/shard_map/conv_general_dilated | solution.py:35
  171.7 4.3 %select_convert_fusion = bf16[8,32,8,3,32]{4,2,3,1,0:T(8,128)(2,1)S(1)} fusion(pred[8,3]{0,1:T(4,128)(4,1)S(1)} %copy-done.12, bf16[3,3,3,32,32]{4,3,2,1,0:T(8,128)(2,1)S(1)} %copy-done.9, bf16[10,34,1,7,2,32]{5,3,4,1,0,2:T(8,128)(2,1)S(1)} %slice.89, bf16[10,34,1,8,3,32]{5,3,4,1,0,2:T(8,128)(2,1)S(1)} %copy-done.4), kind=kOutput, calls=%fused_computation.37 | convolution fusion | flops 342743040 | bytes 1275416 | tf_op jit(solution)/shard_map/conv_general_dilated | solution.py:35
  176.5 1.4 copy.128
  (107 shorter events, 16.3 us)
Async XLA Ops:
  0.0 57.7 %copy-start = (bf16[256,512]{1,0:T(8,128)(2,1)S(1)}, bf16[256,512]{1,0:T(8,128)(2,1)}, u32[]{:S(2)}) copy-start(bf16[256,512]{1,0:T(8,128)(2,1)} %param.15) | copy-start | bytes 786436
  2.0 6.1 %collective-permute-start = (bf16[8,32,1,32]{1,3,2,0:T(8,128)(2,1)S(1)}, bf16[8,32,1,32]{1,3,2,0:T(8,128)(2,1)S(1)}, u32[]{:S(2)}, u32[]{:S(2)}) collective-permute-start(bf16[8,32,1,32]{1,3,2,0:T(8,128)(2,1)S(1)} %get-tuple-element.184), channel_id=1, source_target_pairs={{0,1},{1,2},{2,3},{3,4},{4,5},{5,6},{6,7},{8,9},{9,10},{10,11},{11... | collective-permute-start | bytes 49160 | tf_op jit(solution)/shard_map/ppermute | solution.py:14
  6.8 5.0 %collective-permute-start.1 = (bf16[8,32,1,32]{1,3,2,0:T(8,128)(2,1)S(1)}, bf16[8,32,1,32]{1,3,2,0:T(8,128)(2,1)S(1)}, u32[]{:S(2)}, u32[]{:S(2)}) collective-permute-start(bf16[8,32,1,32]{1,3,2,0:T(8,128)(2,1)S(1)} %get-tuple-element.185), channel_id=1, source_target_pairs={{1,0},{2,1},{3,2},{4,3},{5,4},{6,5},{7,6},{9,8},{10,9},{11,10},{12... | collective-permute-start | bytes 49160 | tf_op jit(solution)/shard_map/ppermute | solution.py:14
  15.9 10.7 %collective-permute-start.2 = (bf16[8,1,18,32]{3,0,2,1:T(8,128)(2,1)S(1)}, bf16[8,1,18,32]{3,0,2,1:T(8,128)(2,1)S(1)}, u32[]{:S(2)}, u32[]{:S(2)}) collective-permute-start(bf16[8,1,18,32]{3,0,2,1:T(8,128)(2,1)S(1)} %copy.106), channel_id=1, source_target_pairs={{0,8},{8,16},{16,24},{24,32},{32,40},{40,48},{48,56},{1,9},{9,17},... | collective-permute-start | bytes 27656 | tf_op jit(solution)/shard_map/ppermute | solution.py:14
  24.6 6.2 %collective-permute-start.3 = (bf16[8,1,18,32]{3,0,2,1:T(8,128)(2,1)S(1)}, bf16[8,1,18,32]{3,0,2,1:T(8,128)(2,1)S(1)}, u32[]{:S(2)}, u32[]{:S(2)}) collective-permute-start(bf16[8,1,18,32]{3,0,2,1:T(8,128)(2,1)S(1)} %copy.107), channel_id=1, source_target_pairs={{8,0},{16,8},{24,16},{32,24},{40,32},{48,40},{56,48},{9,1},{17,9},... | collective-permute-start | bytes 27656 | tf_op jit(solution)/shard_map/ppermute | solution.py:14
  32.8 10.5 %copy-start.1 = (bf16[8,1,18,32]{1,3,2,0:T(8,128)(2,1)S(1)}, bf16[8,1,18,32]{1,3,2,0:T(8,128)(2,1)}, u32[]{:S(2)}) copy-start(bf16[8,1,18,32]{1,3,2,0:T(8,128)(2,1)} %copy.109) | copy-start | bytes 27652
  34.1 5.3 %collective-permute-start.4 = (bf16[1,34,18,32]{1,3,2,0:T(8,128)(2,1)S(1)}, bf16[1,34,18,32]{1,3,2,0:T(8,128)(2,1)S(1)}, u32[]{:S(2)}, u32[]{:S(2)}) collective-permute-start(bf16[1,34,18,32]{1,3,2,0:T(8,128)(2,1)S(1)} %get-tuple-element.174), channel_id=1, source_target_pairs={{0,64},{64,128},{128,192},{192,256},{256,320},{320,384},{384,448},... | collective-permute-start | bytes 117512 | tf_op jit(solution)/shard_map/ppermute | solution.py:14
  37.3 5.9 %collective-permute-start.5 = (bf16[1,34,18,32]{1,3,2,0:T(8,128)(2,1)S(1)}, bf16[1,34,18,32]{1,3,2,0:T(8,128)(2,1)S(1)}, u32[]{:S(2)}, u32[]{:S(2)}) collective-permute-start(bf16[1,34,18,32]{1,3,2,0:T(8,128)(2,1)S(1)} %get-tuple-element.175), channel_id=1, source_target_pairs={{64,0},{128,64},{192,128},{256,192},{320,256},{384,320},{448,384},... | collective-permute-start | bytes 117512 | tf_op jit(solution)/shard_map/ppermute | solution.py:14
  47.8 2.0 %copy-start.5 = (bf16[10,34,1,8,3,32]{5,3,4,1,0,2:T(8,128)(2,1)S(1)}, bf16[10,34,1,8,3,32]{5,3,4,1,0,2:T(8,128)(2,1)}, u32[]{:S(2)}) copy-start(bf16[10,34,1,8,3,32]{5,3,4,1,0,2:T(8,128)(2,1)} %copy.111) | copy-start | bytes 1566724
  47.9 2.0 %copy-start.8 = (bf16[3,3,3,32,32]{4,3,2,1,0:T(8,128)(2,1)S(1)}, bf16[3,3,3,32,32]{4,3,2,1,0:T(8,128)(2,1)}, u32[]{:S(2)}) copy-start(bf16[3,3,3,32,32]{4,3,2,1,0:T(8,128)(2,1)} %param.11) | copy-start | bytes 165892
  47.9 2.0 %copy-start.12 = (pred[8,3]{0,1:T(4,128)(4,1)S(1)}, pred[8,3]{0,1:T(4,128)(4,1)}, u32[]{:S(2)}) copy-start(pred[8,3]{0,1:T(4,128)(4,1)} %constant.79) | copy-start | bytes 76
  54.5 1.2 copy-start.2
  55.7 1.7 copy-start.10
  55.7 1.7 copy-start.11
  69.6 37.7 %all-to-all-start.1 = ((bf16[64,2,2048]{2,1,0:T(2,128)(2,1)}), bf16[64,2,2048]{2,1,0:T(2,128)(2,1)S(1)}, u32[]{:S(2)}, u32[]{:S(2)}) async-start(bf16[64,2,2048]{2,1,0:T(2,128)(2,1)} %reshape.201), calls=%async_computation.1 | async-start | bytes 1048576 | tf_op jit(solution)/shard_map/all_to_all | solution.py:25
  109.1 20.7 %copy-start.6 = (bf16[256,256]{1,0:T(8,128)(2,1)S(1)}, bf16[256,256]{1,0:T(8,128)(2,1)}, u32[]{:S(2)}) copy-start(bf16[256,256]{1,0:T(8,128)(2,1)} %param.17) | copy-start | bytes 393220
  109.1 20.7 %copy-start.7 = (bf16[256,256]{1,0:T(8,128)(2,1)S(1)}, bf16[256,256]{1,0:T(8,128)(2,1)}, u32[]{:S(2)}) copy-start(bf16[256,256]{1,0:T(8,128)(2,1)} %param.16) | copy-start | bytes 393220
  120.7 9.9 %copy-start.3 = (bf16[8,32,8,3,32]{4,1,3,2,0:T(8,128)(2,1)S(1)}, bf16[8,32,8,3,32]{4,1,3,2,0:T(8,128)(2,1)}, u32[]{:S(2)}) copy-start(bf16[8,32,8,3,32]{4,1,3,2,0:T(8,128)(2,1)} %copy-done.2) | copy-start | bytes 1179652
  131.0 3.5 %collective-permute-start.6 = (bf16[8,32,1,32]{3,1,2,0:T(8,128)(2,1)S(1)}, bf16[8,32,1,32]{3,1,2,0:T(8,128)(2,1)S(1)}, u32[]{:S(2)}, u32[]{:S(2)}) collective-permute-start(bf16[8,32,1,32]{3,1,2,0:T(8,128)(2,1)S(1)} %get-tuple-element.182), channel_id=1, source_target_pairs={{0,1},{1,2},{2,3},{3,4},{4,5},{5,6},{6,7},{8,9},{9,10},{10,11},{11... | collective-permute-start | bytes 49160 | tf_op jit(solution)/shard_map/ppermute | solution.py:14
  133.2 5.2 %collective-permute-start.7 = (bf16[8,32,1,32]{3,1,2,0:T(8,128)(2,1)S(1)}, bf16[8,32,1,32]{3,1,2,0:T(8,128)(2,1)S(1)}, u32[]{:S(2)}, u32[]{:S(2)}) collective-permute-start(bf16[8,32,1,32]{3,1,2,0:T(8,128)(2,1)S(1)} %get-tuple-element.183), channel_id=1, source_target_pairs={{1,0},{2,1},{3,2},{4,3},{5,4},{6,5},{7,6},{9,8},{10,9},{11,10},{12... | collective-permute-start | bytes 49160 | tf_op jit(solution)/shard_map/ppermute | solution.py:14
  138.6 8.1 %collective-permute-start.8 = (bf16[8,1,18,32]{3,1,2,0:T(2,128)(2,1)S(1)}, bf16[8,1,18,32]{3,1,2,0:T(2,128)(2,1)S(1)}, u32[]{:S(2)}, u32[]{:S(2)}) collective-permute-start(bf16[8,1,18,32]{3,1,2,0:T(2,128)(2,1)S(1)} %get-tuple-element.178), channel_id=1, source_target_pairs={{0,8},{8,16},{16,24},{24,32},{32,40},{40,48},{48,56},{1,9},{9,17},... | collective-permute-start | bytes 27656 | tf_op jit(solution)/shard_map/ppermute | solution.py:14
  144.8 6.6 %collective-permute-start.9 = (bf16[8,1,18,32]{3,1,2,0:T(2,128)(2,1)S(1)}, bf16[8,1,18,32]{3,1,2,0:T(2,128)(2,1)S(1)}, u32[]{:S(2)}, u32[]{:S(2)}) collective-permute-start(bf16[8,1,18,32]{3,1,2,0:T(2,128)(2,1)S(1)} %get-tuple-element.179), channel_id=1, source_target_pairs={{8,0},{16,8},{24,16},{32,24},{40,32},{48,40},{56,48},{9,1},{17,9},... | collective-permute-start | bytes 27656 | tf_op jit(solution)/shard_map/ppermute | solution.py:14
  151.5 5.4 %collective-permute-start.10 = (bf16[1,34,18,32]{3,1,2,0:T(8,128)(2,1)S(1)}, bf16[1,34,18,32]{3,1,2,0:T(8,128)(2,1)S(1)}, u32[]{:S(2)}, u32[]{:S(2)}) collective-permute-start(bf16[1,34,18,32]{3,1,2,0:T(8,128)(2,1)S(1)} %get-tuple-element.176), channel_id=1, source_target_pairs={{0,64},{64,128},{128,192},{192,256},{256,320},{320,384},{384,448},... | collective-permute-start | bytes 117512 | tf_op jit(solution)/shard_map/ppermute | solution.py:14
  154.4 6.3 %collective-permute-start.11 = (bf16[1,34,18,32]{3,1,2,0:T(8,128)(2,1)S(1)}, bf16[1,34,18,32]{3,1,2,0:T(8,128)(2,1)S(1)}, u32[]{:S(2)}, u32[]{:S(2)}) collective-permute-start(bf16[1,34,18,32]{3,1,2,0:T(8,128)(2,1)S(1)} %get-tuple-element.177), channel_id=1, source_target_pairs={{64,0},{128,64},{192,128},{256,192},{320,256},{384,320},{448,384},... | collective-permute-start | bytes 117512 | tf_op jit(solution)/shard_map/ppermute | solution.py:14
  169.7 2.0 %copy-start.4 = (bf16[10,34,1,8,3,32]{5,3,4,1,0,2:T(8,128)(2,1)S(1)}, bf16[10,34,1,8,3,32]{5,3,4,1,0,2:T(8,128)(2,1)}, u32[]{:S(2)}) copy-start(bf16[10,34,1,8,3,32]{5,3,4,1,0,2:T(8,128)(2,1)} %copy.126) | copy-start | bytes 1566724
  169.7 2.0 %copy-start.9 = (bf16[3,3,3,32,32]{4,3,2,1,0:T(8,128)(2,1)S(1)}, bf16[3,3,3,32,32]{4,3,2,1,0:T(8,128)(2,1)}, u32[]{:S(2)}) copy-start(bf16[3,3,3,32,32]{4,3,2,1,0:T(8,128)(2,1)} %param.12) | copy-start | bytes 165892
where the time goes:
time: 179 us; the launch traced here: 178 us
  starting transfers between devices  54.4 us (30%)
  waiting for transfers between devices  44.4 us (25%)
  local copies, waits for them, and re-layouts  38.2 us (21%)
  blocking collectives  16.8 us (9%)
  matrix products  15.4 us (9%)
  other arithmetic  7.94 us (4%)
    ppermute x12, starting transfers between devices, from_behind(): return lax.ppermute(array, axis, pairs)  36.3 us
    ppermute x12, waiting for transfers between devices, from_behind(): return lax.ppermute(array, axis, pairs)  24.9 us
    all_to_all x1, waiting for transfers between devices, copy_for_each(): lax.all_to_all(jnp.broadcast_to(array[None], (devices, *array.shape)), ax...  19.5 us
    all_to_all x1, starting transfers between devices, copy_for_each(): lax.all_to_all(jnp.broadcast_to(array[None], (devices, *array.shape)), ax...  18.1 us
    unnamed x38, local copies, waits for them, and re-layouts  10.4 us
    conv_general_dilated x4, local copies, waits for them, and re-layouts, convolve(): lax.conv_general_dilated(padded[None], kernel, (1, 1, 1), 'VALID', dimens...  9.89 us
    all_to_all x1, blocking collectives, on_device(): lax.all_to_all(packed, 'gz', split_axis=1, concat_axis=2, tiled=True)  9.49 us
    conv_general_dilated x2, matrix products, convolve(): lax.conv_general_dilated(padded[None], kernel, (1, 1, 1), 'VALID', dimens...  8.72 us
  transfers between devices with their start and end apart: 13, of which 9 were waited for; matrix products, arithmetic and copies ran while one was open for 1% of the time, Pallas kernels for 0%

commit v1 on v0

v1 whole, which is shorter than its diff:
```python
import functools

import jax
import jax.numpy as jnp
from jax import lax
from jax.experimental import pallas as pl
from jax.experimental.pallas import tpu as pltpu
from jax.sharding import PartitionSpec as P

BF = jnp.bfloat16
F32 = jnp.float32
MESH = pl.DeviceIdType.MESH
STEPS = [(a, b, c) for a in (-1, 0, 1) for b in (-1, 0, 1) for c in (-1, 0, 1) if (a, b, c) != (0, 0, 0)]


def iota(shape, dim):
    return lax.broadcasted_iota(jnp.int32, shape, dim)


def dot(left, right):
    return jnp.dot(left, right, preferred_element_type=F32)


def roll(value, shift, axis):
    return pltpu.roll(value, shift, axis)


def lane_window(c, width):
    if c == 0:
        return (0, 512), (128, 512)
    if c == 1:
        return (384, 128), (0, 128)
    return (0, 128), (640, 128)


def kernel(sizes, x_hbm, win_hbm, wout_hbm, gain_hbm, qw_hbm, kvw_hbm, ow_hbm, uw_hbm, out_ref,
           vol, vol_lo, vol_hi, enc, enc_lo, enc_hi, joi, joi_lo, joi_hi, rows_v, rows_e,
           win, wout, gain, qw, kvw, ow, uw, taps, lhs, acc, tokens_s,
           qbuf, kvbuf, kmask, vmask, osend, orecv, lsend, lrecv, up, uppad,
           load_sem, vs, vr, es, er, us, ur, gs, gr, rs, rr):
    GX, GY, GZ = sizes
    gx, gy, gz = lax.axis_index("gx"), lax.axis_index("gy"), lax.axis_index("gz")
    n_row, n_col = (GY // 2) * GZ, GX * 2

    def at_mesh(x, y, z):
        return (x, y, z)

    def row_peer(i, sign=1):
        return at_mesh(gx, (gy + GY + sign * 2 * (i // GZ)) % GY, (gz + GZ + sign * (i % GZ)) % GZ)

    def col_peer(i):
        return at_mesh((gx + i // 2) % GX, gy // 2 * 2 + (gy + i % 2) % 2, gz)

    def inside(a, b, c):
        ok = None
        for at, step, size in ((gx, a, GX), (gy, b, GY), (gz, c, GZ)):
            if step:
                here = at < size - 1 if step > 0 else at > 0
                ok = here if ok is None else ok & here
        return ok

    def neighbour(a, b, c):
        return at_mesh(gx + a, gy + b, gz + c)

    for ref in (vol, enc, vol_lo, vol_hi, enc_lo, enc_hi, uppad):
        ref[...] = jnp.zeros(ref.shape, ref.dtype)
    barrier = pltpu.get_barrier_semaphore()
    for step in STEPS:
        @pl.when(inside(*step))
        def _(step=step):
            pl.semaphore_signal(barrier, inc=1, device_id=neighbour(*step), device_id_type=MESH)
    for i in range(1, n_row):
        pl.semaphore_signal(barrier, inc=1, device_id=row_peer(i), device_id_type=MESH)
    for i in range(1, n_col):
        pl.semaphore_signal(barrier, inc=1, device_id=col_peer(i), device_id_type=MESH)

    own = (pl.ds(1, 8), pl.ds(0, 32), pl.ds(128, 512))
    loads = [pltpu.make_async_copy(x_hbm, vol.at[own], load_sem.at[0])]
    pairs = [(win_hbm, win), (wout_hbm, wout), (gain_hbm, gain), (qw_hbm, qw), (kvw_hbm, kvw), (ow_hbm, ow), (uw_hbm, uw)]
    loads += [pltpu.make_async_copy(s, d, load_sem.at[i + 1]) for i, (s, d) in enumerate(pairs)]
    for copy in loads:
        copy.start()

    def pack_rows(main, rows):
        r, k = iota((32, 256), 0), iota((32, 256), 1)
        wanted = jnp.where(r < 16, r * 32, (r - 16) * 32 + 31)
        picked = dot((wanted == k).astype(F32).astype(BF), main[own].reshape(256, 512))
        rows[...] = picked.astype(BF).reshape(2, 16, 512)

    def remote(src, dst, send, recv, step):
        copy = pltpu.make_async_remote_copy(src_ref=src, dst_ref=dst, send_sem=send, recv_sem=recv,
                                            device_id=neighbour(*step), device_id_type=MESH)
        return copy, pltpu.make_async_copy(dst, dst, recv), pltpu.make_async_copy(src, src, send)

    def halo_copies(main, rows, lo, hi, send, recv):
        copies = []
        for n, (a, b, c) in enumerate(STEPS):
            (s0, width), (d0, _) = lane_window(c, 512)
            if b == 0:
                sx = {-1: pl.ds(1, 1), 0: pl.ds(1, 8), 1: pl.ds(8, 1)}[a]
                dx = {-1: pl.ds(9, 1), 0: pl.ds(1, 8), 1: pl.ds(0, 1)}[a]
                src = main.at[sx, pl.ds(0, 32), pl.ds(128 + s0, width)]
                dst = main.at[dx, pl.ds(0, 32), pl.ds(d0, width)]
            else:
                src = rows.at[1 if b == 1 else 0, pl.ds(0, 16), pl.ds(s0, width)]
                dst = (lo if b == 1 else hi).at[1 - a, pl.ds(0, 16), pl.ds(d0, width)]
            copies.append(remote(src, dst, send.at[n], recv.at[n], (a, b, c)))
        return copies

    def start_all(copies):
        for step, (copy, _, _) in zip(STEPS, copies):
            @pl.when(inside(*step))
            def _(copy=copy):
                copy.start()

    def arrived(copies):
        for (a, b, c), (_, landing, _) in zip(STEPS, copies):
            @pl.when(inside(-a, -b, -c))
            def _(landing=landing):
                landing.wait()

    def departed(copies):
        for step, (_, _, leaving) in zip(STEPS, copies):
            @pl.when(inside(*step))
            def _(leaving=leaving):
                leaving.wait()

    def spread_taps(w):
        k, n = iota((32, 512), 0), iota((32, 512), 1)
        place = ((n % 32 == k) & (n // 128 == (n % 128) // 32)).astype(F32).astype(BF)
        moved = dot(w[...], place).astype(BF)
        taps[...] = jnp.zeros(taps.shape, BF)
        for dx in range(3):
            for dy in range(3):
                first = (dx * 3 + dy) * 96
                for m in range(2):
                    for block in range(6):
                        total = None
                        for g in range(4):
                            dz = block - g
                            if 0 <= dz <= 2:
                                piece = moved[first + dz * 32:first + dz * 32 + 32, g * 128:g * 128 + 128]
                                total = piece if total is None else total + piece
                        r0 = dx * 512 + (4 * m + 3 + block) * 32
                        taps[dy, r0:r0 + 32, m * 128:m * 128 + 128] = total

    def convolve(main, lo, hi, emit):
        row8 = iota((8, 768), 0)

        def three(rim):
            before, here, after = (rim[i].astype(F32)[0:8] for i in range(3))
            return (jnp.where(row8 == 0, roll(before, 1, 0), roll(here, 1, 0)), here,
                    jnp.where(row8 == 7, roll(after, 7, 0), roll(here, 7, 0)))

        rims = [jnp.concatenate(p, axis=0).astype(BF) for p in zip(three(lo), three(hi))]
        for dx in range(3):
            for h in range(2):
                lhs[h * 256:h * 256 + 256, dx * 512:dx * 512 + 512] = main[dx:dx + 8, :, h * 256:h * 256 + 512].reshape(256, 512)
                lhs[512 + 16 * h:528 + 16 * h, dx * 512:dx * 512 + 512] = rims[dx][:, h * 256:h * 256 + 512]

        def one(dy, carry):
            acc[dy, 0:544, :] = dot(lhs[...], taps[dy])
            return carry

        lax.fori_loop(0, 3, one, 0)
        row = iota((32, 256), 0)

        def join(x, carry):
            for h in range(2):
                at = pl.ds(pl.multiple_of(h * 256 + x * 32, 32), 32)
                below = jnp.where(row == 0, acc[0, pl.ds(512 + 16 * h + x, 1), :], roll(acc[0, at, :], 1, 0))
                above = jnp.where(row == 31, acc[2, pl.ds(520 + 16 * h + x, 1), :], roll(acc[2, at, :], 31, 0))
                emit(x, h, below + acc[1, at, :] + above)
            return carry

        lax.fori_loop(0, 8, join, 0)

    loads[0].wait()
    pack_rows(vol, rows_v)
    neighbours = (1 + (gx > 0).astype(jnp.int32) + (gx < GX - 1).astype(jnp.int32))
    neighbours *= (1 + (gy > 0).astype(jnp.int32) + (gy < GY - 1).astype(jnp.int32))
    neighbours *= (1 + (gz > 0).astype(jnp.int32) + (gz < GZ - 1).astype(jnp.int32))
    pl.semaphore_wait(barrier, neighbours - 1 + n_row - 1 + n_col - 1)
    vol_copies = halo_copies(vol, rows_v, vol_lo, vol_hi, vs, vr)
    start_all(vol_copies)
    for copy in loads[1:]:
        copy.wait()
    spread_taps(win)
    arrived(vol_copies)

    def keep_encoded(x, h, value):
        enc[1 + x, :, 128 + 256 * h:384 + 256 * h] = jnp.maximum(value, 0.0).astype(BF)

    convolve(vol, vol_lo, vol_hi, keep_encoded)

    r, k = iota((32, 256), 0), iota((32, 256), 1)
    pool = ((k // 128 == r // 16) & ((k % 32) // 4 == 2 * (r % 4) + (r // 8) % 2)).astype(F32).astype(BF)
    sums = dot(pool, enc[own].reshape(256, 512))
    row8, group8 = iota((8, 128), 0), iota((8, 128), 1) // 32
    chunks = []
    for q in range(4):
        part = sums[:, q * 128:q * 128 + 128]
        part = part + roll(part, 64, 1)
        chunks.append(part + roll(part, 32, 1))

    def cell(ab, c):
        return jnp.where(row8 < 4, chunks[c][ab * 8:ab * 8 + 8], chunks[2 + c][ab * 8:ab * 8 + 8])

    sides = []
    for a in range(2):
        side = cell(2 * a + 1, 1)
        for n, (b, c) in enumerate(((0, 0), (0, 1), (1, 0))):
            side = jnp.where(group8 == n, cell(2 * a + b, c), side)
        sides.append(side)
    tokens = jnp.concatenate(sides, axis=1) * (1.0 / 64.0)
    tokens_s[...] = tokens
    center = tokens - jnp.mean(tokens, axis=1, keepdims=True)
    variance = jnp.mean(center * center, axis=1, keepdims=True)
    normed = center * lax.rsqrt(variance + 1e-05) * gain[...]
    normed = jnp.concatenate([normed, jnp.zeros_like(normed)], axis=0).astype(BF)
    queries = dot(normed, qw[...])[0:8]
    key_value = dot(normed, kvw[...])[0:8]
    qbuf[0] = jnp.concatenate([queries[:, i * 128:i * 128 + 128] for i in range(2)], axis=0).astype(BF)
    kvbuf[0] = jnp.concatenate([key_value[:, i * 128:i * 128 + 128] for i in range(4)], axis=0).astype(BF)

    q_all = pltpu.make_async_copy(qbuf.at[pl.ds(1, n_row - 1)], qbuf.at[pl.ds(1, n_row - 1)], gr.at[0])
    kv_all = pltpu.make_async_copy(kvbuf.at[pl.ds(1, n_col - 1)], kvbuf.at[pl.ds(1, n_col - 1)], gr.at[1])
    q_gone = pltpu.make_async_copy(qbuf.at[pl.ds(1, n_row - 1)], qbuf.at[pl.ds(1, n_row - 1)], gs.at[0])
    kv_gone = pltpu.make_async_copy(kvbuf.at[pl.ds(1, n_col - 1)], kvbuf.at[pl.ds(1, n_col - 1)], gs.at[1])
    for i in range(n_row - 1, 0, -1):
        pltpu.make_async_remote_copy(src_ref=qbuf.at[0], dst_ref=qbuf.at[i], send_sem=gs.at[0], recv_sem=gr.at[0],
                                     device_id=row_peer(i), device_id_type=MESH).start()
    for i in range(n_col - 1, 0, -1):
        pltpu.make_async_remote_copy(src_ref=kvbuf.at[0], dst_ref=kvbuf.at[i], send_sem=gs.at[1], recv_sem=gr.at[1],
                                     device_id=col_peer(i), device_id_type=MESH).start()
    pack_rows(enc, rows_e)
    enc_copies = halo_copies(enc, rows_e, enc_lo, enc_hi, es, er)
    start_all(enc_copies)
    spread_taps(wout)

    q_all.wait()
    kv_all.wait()
    n_keys = n_col * 16
    lane_group = iota((n_keys, 128), 1) // 32
    keys = kvbuf[:, 0:16, :].reshape(n_keys, 128)
    values = kvbuf[:, 16:32, :].reshape(n_keys, 128)
    for g in range(4):
        mine = (lane_group == g).astype(F32).astype(BF)
        kmask[g] = keys * mine
        vmask[g, :, 0:128] = values * mine
        vmask[g, :, 128:256] = mine
    slots = min(8, n_row)
    n_rows = slots * 16
    same_half = (iota((n_rows, n_keys), 0) // 8) % 2 == (iota((n_rows, n_keys), 1) // 8) % 2
    group = iota((n_rows, 128), 1) // 32
    compact = iota((slots, 16, 128), 1) == iota((slots, 16, 128), 2) % 32

    def attend(i, carry):
        at = pl.ds(i * slots, slots)
        query = qbuf[at].reshape(n_rows, 128)
        total, peaks = jnp.zeros((n_rows, 256), F32), jnp.zeros((n_rows, 128), F32)
        for g in range(4):
            scores = lax.dot_general(query, kmask[g], (((1,), (1,)), ((), ())), preferred_element_type=F32)
            scores = jnp.where(same_half, scores * 32 ** (-0.5), -1e30)
            peak = jnp.max(scores, axis=1, keepdims=True)
            total = total + dot(jnp.exp(scores - peak).astype(BF), vmask[g])
            peaks = jnp.where(group == g, peak, peaks)
        weight = total[:, 128:256]
        osend[at] = (total[:, 0:128] / weight).astype(BF).reshape(slots, 16, 128)
        level = (peaks + jnp.log(weight)).reshape(slots, 16, 128)
        lsend[at] = jnp.sum(jnp.where(compact, level, 0.0), axis=1, keepdims=True)
        return carry

    lax.fori_loop(0, n_row // slots, attend, 0)
    others = pl.ds(1, n_row - 1)
    for i in range(n_row - 1, 0, -1):
        pltpu.make_async_remote_copy(src_ref=lsend.at[i], dst_ref=lrecv.at[i], send_sem=rs.at[1], recv_sem=rr.at[1],
                                     device_id=row_peer(i, -1), device_id_type=MESH).start()
        pltpu.make_async_remote_copy(src_ref=osend.at[i], dst_ref=orecv.at[i], send_sem=rs.at[0], recv_sem=rr.at[0],
                                     device_id=row_peer(i, -1), device_id_type=MESH).start()
    orecv[0] = osend[0]
    lrecv[0] = lsend[0]
    arrived(enc_copies)
    pltpu.make_async_copy(orecv.at[others], orecv.at[others], rr.at[0]).wait()
    pltpu.make_async_copy(lrecv.at[others], lrecv.at[others], rr.at[1]).wait()

    levels = lrecv[...]
    share = jnp.exp(levels - jnp.max(levels, axis=0, keepdims=True))
    share = share / jnp.sum(share, axis=0, keepdims=True)
    spot = iota((n_row, 16, 128), 1) == iota((n_row, 16, 128), 2) % 32
    share = jnp.where(spot, share, 0.0).reshape(n_row * 16, 128)
    high = share.astype(BF)
    low = (share - high.astype(F32)).astype(BF)
    blocks = ((iota((256, 128), 0) % 128) // 32 == iota((256, 128), 1) // 32).astype(F32).astype(BF)
    share = dot(jnp.concatenate([high, low], axis=1), blocks).reshape(n_row, 16, 128)
    attended = jnp.sum(share * orecv[...].astype(F32), axis=0)
    attended = jnp.concatenate([attended[0:8], attended[8:16]], axis=1)
    attended = jnp.concatenate([attended, jnp.zeros_like(attended)], axis=0).astype(BF)
    mixture = tokens_s[...] + dot(attended, ow[...])[0:8]
    mixture = jnp.concatenate([mixture, jnp.zeros_like(mixture)], axis=0).astype(BF)
    r, k = iota((16, 16), 0), iota((16, 16), 1)
    twice = ((r // 8) * 4 + (r % 8) // 2 == k).astype(F32).astype(BF)
    upward = dot(dot(twice, mixture).astype(BF), uw[...])
    odd, right = row8 % 2 == 1, group8 >= 2
    for a in range(2):
        first = upward[0:8, a * 128:a * 128 + 128]
        second = upward[8:16, a * 128:a * 128 + 128]
        plane = jnp.where(right, jnp.where(odd, second, roll(second, 64, 1)), jnp.where(odd, roll(first, 64, 1), first))
        for y in range(8):
            up[a, y, 0] = plane[y:y + 1, :]
            uppad[1 + a, 1 + y, 1] = plane[y:y + 1, :]

    up_copies = []
    for n, (a, b, c) in enumerate(STEPS):
        sx = {-1: pl.ds(0, 1), 0: pl.ds(0, 2), 1: pl.ds(1, 1)}[a]
        dx = {-1: pl.ds(3, 1), 0: pl.ds(1, 2), 1: pl.ds(0, 1)}[a]
        sy = {-1: pl.ds(0, 1), 0: pl.ds(0, 8), 1: pl.ds(7, 1)}[b]
        dy = {-1: pl.ds(9, 1), 0: pl.ds(1, 8), 1: pl.ds(0, 1)}[b]
        up_copies.append(remote(up.at[sx, sy, pl.ds(0, 1)], uppad.at[dx, dy, pl.ds(1 - c, 1)], us.at[n], ur.at[n], (a, b, c)))
    start_all(up_copies)
    arrived(up_copies)

    group1 = iota((1, 128), 1) // 32

    def wide(plane, y):
        middle = uppad[plane, y, 1]
        parts = [uppad[plane, y, 0]]
        for q in range(4):
            part = jnp.where(group1 == q, middle, 0.0)
            part = part + roll(part, 64, 1)
            parts.append(part + roll(part, 32, 1))
        return jnp.concatenate(parts + [uppad[plane, y, 2]], axis=1)

    row_wide = iota((8, 768), 0)
    for plane in range(4):
        xs = (range(0, 1), range(1, 5), range(5, 9), range(9, 10))[plane]
        for y2 in range(2):
            four = [wide(plane, 1 + 4 * y2 + i) for i in range(4)]
            more = jnp.concatenate([jnp.where(row_wide < 4, four[2 * i], four[2 * i + 1]) for i in range(2)], axis=0)
            for x in xs:
                joi[x, 16 * y2:16 * y2 + 16, :] = (enc[x, 16 * y2:16 * y2 + 16, :].astype(F32) + more).astype(BF)
    row_rim = iota((16, 768), 0)
    for rim, full, y in ((enc_lo, joi_lo, 0), (enc_hi, joi_hi, 9)):
        planes = [wide(plane, y) for plane in range(4)]
        full[0] = (rim[0].astype(F32) + planes[0]).astype(BF)
        full[1] = (rim[1].astype(F32) + jnp.where(row_rim < 4, planes[1], planes[2])).astype(BF)
        full[2] = (rim[2].astype(F32) + planes[3]).astype(BF)

    def keep_result(x, h, value):
        out_ref[x, :, 256 * h:256 * h + 256] = value.astype(BF)

    convolve(joi, joi_lo, joi_hi, keep_result)

    departed(vol_copies)
    departed(enc_copies)
    departed(up_copies)
    q_gone.wait()
    kv_gone.wait()
    pltpu.make_async_copy(orecv.at[others], orecv.at[others], rs.at[0]).wait()
    pltpu.make_async_copy(lrecv.at[others], lrecv.at[others], rs.at[1]).wait()


def on_device(sizes, volume, conv_in, conv_out, norm_gain, q_weight, kv_weight, out_weight, up_weight):
    n_row, n_col = (sizes[1] // 2) * sizes[2], sizes[0] * 2
    wide = volume.reshape(8, 32, 512)
    padded, rim, rows = (10, 32, 768), (3, 16, 768), (2, 16, 512)
    vmem = pltpu.VMEM
    scratch = [vmem(padded, BF), vmem(rim, BF), vmem(rim, BF)] * 3 + [vmem(rows, BF)] * 2
    scratch += [vmem((864, 32), BF)] * 2 + [vmem((1, 256), F32), vmem((256, 256), BF), vmem((256, 512), BF), vmem((256, 256), BF), vmem((256, 256), BF)]
    scratch += [vmem((3, 1536, 256), BF), vmem((544, 1536), BF), vmem((3, 552, 256), F32), vmem((8, 256), F32)]
    scratch += [vmem((n_row, 16, 128), BF), vmem((n_col, 32, 128), BF), vmem((4, n_col * 16, 128), BF), vmem((4, n_col * 16, 256), BF)]
    scratch += [vmem((n_row, 16, 128), BF)] * 2 + [vmem((n_row, 1, 128), F32)] * 2
    scratch += [vmem((2, 8, 1, 1, 128), F32), vmem((4, 10, 3, 1, 128), F32)]
    dma = pltpu.SemaphoreType.DMA
    scratch += [dma((8,))] + [dma((26,))] * 6 + [dma((2,))] * 4
    result = pl.pallas_call(
        functools.partial(kernel, sizes),
        out_shape=jax.ShapeDtypeStruct((8, 32, 512), BF),
        in_specs=[pl.BlockSpec(memory_space=pl.ANY)] * 8,
        out_specs=pl.BlockSpec(memory_space=pltpu.VMEM),
        scratch_shapes=scratch,
        compiler_params=pltpu.CompilerParams(collective_id=0, has_side_effects=True, vmem_limit_bytes=48 * 2**20),
    )(wide, conv_in.reshape(864, 32), conv_out.reshape(864, 32), norm_gain.reshape(1, 256), q_weight, kv_weight, out_weight, up_weight)
    return result.reshape(8, 32, 16, 32)


def solution(mesh):
    placed = (P("gx", "gy", "gz", None), P(), P(), P(), P(), P(), P(), P())
    sizes = tuple(mesh.shape[name] for name in ("gx", "gy", "gz"))
    return jax.shard_map(
        functools.partial(on_device, sizes), mesh=mesh, in_specs=placed, out_specs=P("gx", "gy", "gz", None), check_vma=False
    )
```

time: 179 us -> 55.6 us (0.31)
  starting transfers between devices: 54.4 us -> 0 us
  Pallas kernels: 0 us -> 51.4 us
  waiting for transfers between devices: 44.4 us -> 0 us
  local copies, waits for them, and re-layouts: 38.2 us -> 3.89 us
  blocking collectives: 16.8 us -> 0 us
  matrix products: 15.4 us -> 0 us
  other arithmetic: 7.94 us -> 0 us
    pallas_call x0 -> x1, Pallas kernels: none -> 51.4 us  [on_device(): pl.pallas_call(functools.partial(kernel, sizes), out_shape=jax.ShapeDtype...]
    ppermute x12 -> x0, starting transfers between devices: 36.3 us -> none  [from_behind(): return lax.ppermute(array, axis, pairs)]
    ppermute x12 -> x0, waiting for transfers between devices: 24.9 us -> none  [from_behind(): return lax.ppermute(array, axis, pairs)]
    all_to_all x1 -> x0, waiting for transfers between devices: 19.5 us -> none  [copy_for_each(): lax.all_to_all(jnp.broadcast_to(array[None], (devices, *array.shape)), ax...]
    all_to_all x1 -> x0, starting transfers between devices: 18.1 us -> none  [copy_for_each(): lax.all_to_all(jnp.broadcast_to(array[None], (devices, *array.shape)), ax...]
    all_to_all x2 -> x0, blocking collectives: 16.8 us -> none  [the longest x1 9.49 us: on_device(): lax.all_to_all(packed, 'gz', split_axis=1, concat_axis=2, tiled=True)]
    unnamed x38 -> x14, local copies, waits for them, and re-layouts: 10.4 us -> 0.03 us
    conv_general_dilated x4 -> x0, local copies, waits for them, and re-layouts: 9.89 us -> none  [convolve(): lax.conv_general_dilated(padded[None], kernel, (1, 1, 1), 'VALID', dimens...]
  transfers between devices with their start and end apart: 13 -> 0, of which waited for: 9 -> 0; matrix products, arithmetic and copies ran while one was open for 1% -> 0% of each run, Pallas kernels for 0% -> 0%
where the time goes in v1:
time: 55.6 us; the launch traced here: 55.4 us
  Pallas kernels  51.4 us (92%)
  local copies, waits for them, and re-layouts  3.89 us (7%)
    pallas_call x1, Pallas kernels, on_device(): pl.pallas_call(functools.partial(kernel, sizes), out_shape=jax.ShapeDtype...  51.4 us
    reshape x1, local copies, waits for them, and re-layouts, on_device(): wide = volume.reshape(8, 32, 512)  2.3 us
    reshape x1, local copies, waits for them, and re-layouts, on_device(): return result.reshape(8, 32, 16, 32)  1.56 us

profile of v1, /device:TPU:1, one launch (start us, length us, event | category | flops | bytes accessed | tf_op | source)
XLA Modules:
  0.0 55.4 jit_solution(16434011998135460446)
XLA Ops:
  0.0 0.0 copy-start
  0.0 0.0 copy-start.1
  0.0 0.0 copy-start.2
  0.0 0.0 copy-start.3
  0.0 0.0 copy-start.4
  0.0 0.0 copy-start.5
  0.0 0.0 copy-start.6
  0.0 2.3 %reshape.15.x_hbm = bf16[8,32,512]{2,1,0:T(8,128)(2,1)S(1)} reshape(bf16[8,32,16,32]{3,2,1,0:T(8,128)(2,1)} %param.8) | data formatting | bytes 524288 | tf_op jit(solution)/shard_map/reshape | solution.py:365
  2.4 0.0 copy-done
  2.4 0.0 copy-done.1
  2.4 0.0 copy-done.2
  2.4 0.0 copy-done.3
  2.4 0.0 copy-done.4
  2.4 0.0 copy-done.5
  2.4 0.0 copy-done.6
  2.4 51.4 %shard_map.82 = bf16[8,32,512]{2,1,0:T(8,128)(2,1)S(1)} custom-call(bf16[8,32,512]{2,1,0:T(8,128)(2,1)S(1)} %reshape.15.x_hbm, bf16[864,32]{1,0:T(8,128)(2,1)S(1)} %bitcast.5, bf16[864,32]{1,0:T(8,128)(2,1)S(1)} %bitcast.6, f32[1,256]{1,0:T(1,128)S(1)} %bitcast.7, bf16[256,256]{1,0:T(8,128)(2,1)S(1)} %copy-done.3, bf16[256,512]{1,0:T(8,128)(2,1)S(1)} %copy-done, ...), custom_call_target="tpu_custom_call" | custom-call | tf_op jit(solution)/shard_map/pallas_call | solution.py:376
  53.9 1.6 %reshape.19 = bf16[8,32,16,32]{3,2,1,0:T(8,128)(2,1)} reshape(bf16[8,32,512]{2,1,0:T(8,128)(2,1)S(1)} %shard_map.82) | data formatting | bytes 524288 | tf_op jit(solution)/shard_map/reshape | solution.py:384
Async XLA Ops:
  0.0 2.4 %copy-start = (bf16[256,512]{1,0:T(8,128)(2,1)S(1)}, bf16[256,512]{1,0:T(8,128)(2,1)}, u32[]{:S(2)}) copy-start(bf16[256,512]{1,0:T(8,128)(2,1)} %kvw_hbm.1) | copy-start | bytes 786436
  0.0 2.4 %copy-start.1 = (bf16[3,3,3,32,32]{4,3,2,1,0:T(8,128)(2,1)S(1)}, bf16[3,3,3,32,32]{4,3,2,1,0:T(8,128)(2,1)}, u32[]{:S(2)}) copy-start(bf16[3,3,3,32,32]{4,3,2,1,0:T(8,128)(2,1)} %param.9) | copy-start | bytes 165892
  0.0 2.4 %copy-start.2 = (bf16[3,3,3,32,32]{4,3,2,1,0:T(8,128)(2,1)S(1)}, bf16[3,3,3,32,32]{4,3,2,1,0:T(8,128)(2,1)}, u32[]{:S(2)}) copy-start(bf16[3,3,3,32,32]{4,3,2,1,0:T(8,128)(2,1)} %param.10) | copy-start | bytes 165892
  0.0 2.4 %copy-start.3 = (bf16[256,256]{1,0:T(8,128)(2,1)S(1)}, bf16[256,256]{1,0:T(8,128)(2,1)}, u32[]{:S(2)}) copy-start(bf16[256,256]{1,0:T(8,128)(2,1)} %qw_hbm.1) | copy-start | bytes 393220
  0.0 2.4 %copy-start.4 = (bf16[256,256]{1,0:T(8,128)(2,1)S(1)}, bf16[256,256]{1,0:T(8,128)(2,1)}, u32[]{:S(2)}) copy-start(bf16[256,256]{1,0:T(8,128)(2,1)} %ow_hbm.1) | copy-start | bytes 393220
  0.0 2.4 %copy-start.5 = (bf16[256,256]{1,0:T(8,128)(2,1)S(1)}, bf16[256,256]{1,0:T(8,128)(2,1)}, u32[]{:S(2)}) copy-start(bf16[256,256]{1,0:T(8,128)(2,1)} %uw_hbm.1) | copy-start | bytes 393220
  0.0 2.4 %copy-start.6 = (f32[256]{0:T(256)S(1)}, f32[256]{0:T(256)}, u32[]{:S(2)}) copy-start(f32[256]{0:T(256)} %param.11) | copy-start | bytes 3076

commit v2 on v1

--- a/solution.py
+++ b/solution.py
@@ -11,6 +11,7 @@
 F32 = jnp.float32
 MESH = pl.DeviceIdType.MESH
 STEPS = [(a, b, c) for a in (-1, 0, 1) for b in (-1, 0, 1) for c in (-1, 0, 1) if (a, b, c) != (0, 0, 0)]
+STEPS.sort(key=lambda step: -sum(abs(v) for v in step))
 
 
 def iota(shape, dim):
@@ -34,7 +35,7 @@
 
 
 def kernel(sizes, x_hbm, win_hbm, wout_hbm, gain_hbm, qw_hbm, kvw_hbm, ow_hbm, uw_hbm, out_ref,
-           vol, vol_lo, vol_hi, enc, enc_lo, enc_hi, joi, joi_lo, joi_hi, rows_v, rows_e,
+           raw, vol, vol_lo, vol_hi, enc, enc_lo, enc_hi, joi, joi_lo, joi_hi, rows_v, rows_e,
            win, wout, gain, qw, kvw, ow, uw, taps, lhs, acc, tokens_s,
            qbuf, kvbuf, kmask, vmask, osend, orecv, lsend, lrecv, up, uppad,
            load_sem, vs, vr, es, er, us, ur, gs, gr, rs, rr):
@@ -50,6 +51,9 @@
 
     def col_peer(i):
         return at_mesh((gx + i // 2) % GX, gy // 2 * 2 + (gy + i % 2) % 2, gz)
+
+    row_far = sorted(range(1, n_row), key=lambda i: -2 * min(i // GZ, GY // 2 - i // GZ) - min(i % GZ // 2, GZ // 2 - i % GZ // 2) - i % 2)
+    col_far = sorted(range(1, n_col), key=lambda i: -min(i // 2, GX - i // 2))
 
     def inside(a, b, c):
         ok = None
@@ -62,7 +66,12 @@
     def neighbour(a, b, c):
         return at_mesh(gx + a, gy + b, gz + c)
 
-    for ref in (vol, enc, vol_lo, vol_hi, enc_lo, enc_hi, uppad):
+    for ref in (vol, enc):
+        for x in (0, 9):
+            ref[x] = jnp.zeros((32, 768), BF)
+        for z in (0, 640):
+            ref[1:9, :, z:z + 128] = jnp.zeros((8, 32, 128), BF)
+    for ref in (vol_lo, vol_hi, enc_lo, enc_hi, uppad):
         ref[...] = jnp.zeros(ref.shape, ref.dtype)
     barrier = pltpu.get_barrier_semaphore()
     for step in STEPS:
@@ -75,7 +84,7 @@
         pl.semaphore_signal(barrier, inc=1, device_id=col_peer(i), device_id_type=MESH)
 
     own = (pl.ds(1, 8), pl.ds(0, 32), pl.ds(128, 512))
-    loads = [pltpu.make_async_copy(x_hbm, vol.at[own], load_sem.at[0])]
+    loads = [pltpu.make_async_copy(x_hbm, raw, load_sem.at[0])]
     pairs = [(win_hbm, win), (wout_hbm, wout), (gain_hbm, gain), (qw_hbm, qw), (kvw_hbm, kvw), (ow_hbm, ow), (uw_hbm, uw)]
     loads += [pltpu.make_async_copy(s, d, load_sem.at[i + 1]) for i, (s, d) in enumerate(pairs)]
     for copy in loads:
@@ -176,6 +185,8 @@
         lax.fori_loop(0, 8, join, 0)
 
     loads[0].wait()
+    for x in range(8):
+        vol[1 + x, :, 128:640] = raw[x].reshape(32, 512)
     pack_rows(vol, rows_v)
     neighbours = (1 + (gx > 0).astype(jnp.int32) + (gx < GX - 1).astype(jnp.int32))
     neighbours *= (1 + (gy > 0).astype(jnp.int32) + (gy < GY - 1).astype(jnp.int32))
@@ -227,10 +238,10 @@
     kv_all = pltpu.make_async_copy(kvbuf.at[pl.ds(1, n_col - 1)], kvbuf.at[pl.ds(1, n_col - 1)], gr.at[1])
     q_gone = pltpu.make_async_copy(qbuf.at[pl.ds(1, n_row - 1)], qbuf.at[pl.ds(1, n_row - 1)], gs.at[0])
     kv_gone = pltpu.make_async_copy(kvbuf.at[pl.ds(1, n_col - 1)], kvbuf.at[pl.ds(1, n_col - 1)], gs.at[1])
-    for i in range(n_row - 1, 0, -1):
+    for i in row_far:
         pltpu.make_async_remote_copy(src_ref=qbuf.at[0], dst_ref=qbuf.at[i], send_sem=gs.at[0], recv_sem=gr.at[0],
                                      device_id=row_peer(i), device_id_type=MESH).start()
-    for i in range(n_col - 1, 0, -1):
+    for i in col_far:
         pltpu.make_async_remote_copy(src_ref=kvbuf.at[0], dst_ref=kvbuf.at[i], send_sem=gs.at[1], recv_sem=gr.at[1],
                                      device_id=col_peer(i), device_id_type=MESH).start()
     pack_rows(enc, rows_e)
@@ -273,7 +284,7 @@
 
     lax.fori_loop(0, n_row // slots, attend, 0)
     others = pl.ds(1, n_row - 1)
-    for i in range(n_row - 1, 0, -1):
+    for i in row_far:
         pltpu.make_async_remote_copy(src_ref=lsend.at[i], dst_ref=lrecv.at[i], send_sem=rs.at[1], recv_sem=rr.at[1],
                                      device_id=row_peer(i, -1), device_id_type=MESH).start()
         pltpu.make_async_remote_copy(src_ref=osend.at[i], dst_ref=orecv.at[i], send_sem=rs.at[0], recv_sem=rr.at[0],
@@ -362,10 +373,9 @@
 
 def on_device(sizes, volume, conv_in, conv_out, norm_gain, q_weight, kv_weight, out_weight, up_weight):
     n_row, n_col = (sizes[1] // 2) * sizes[2], sizes[0] * 2
-    wide = volume.reshape(8, 32, 512)
     padded, rim, rows = (10, 32, 768), (3, 16, 768), (2, 16, 512)
     vmem = pltpu.VMEM
-    scratch = [vmem(padded, BF), vmem(rim, BF), vmem(rim, BF)] * 3 + [vmem(rows, BF)] * 2
+    scratch = [vmem((8, 32, 16, 32), BF)] + [vmem(padded, BF), vmem(rim, BF), vmem(rim, BF)] * 3 + [vmem(rows, BF)] * 2
     scratch += [vmem((864, 32), BF)] * 2 + [vmem((1, 256), F32), vmem((256, 256), BF), vmem((256, 512), BF), vmem((256, 256), BF), vmem((256, 256), BF)]
     scratch += [vmem((3, 1536, 256), BF), vmem((544, 1536), BF), vmem((3, 552, 256), F32), vmem((8, 256), F32)]
     scratch += [vmem((n_row, 16, 128), BF), vmem((n_col, 32, 128), BF), vmem((4, n_col * 16, 128), BF), vmem((4, n_col * 16, 256), BF)]
@@ -376,11 +386,11 @@
     result = pl.pallas_call(
         functools.partial(kernel, sizes),
         out_shape=jax.ShapeDtypeStruct((8, 32, 512), BF),
-        in_specs=[pl.BlockSpec(memory_space=pl.ANY)] * 8,
+        in_specs=[pl.BlockSpec(memory_space=pltpu.HBM)] * 8,
         out_specs=pl.BlockSpec(memory_space=pltpu.VMEM),
         scratch_shapes=scratch,
         compiler_params=pltpu.CompilerParams(collective_id=0, has_side_effects=True, vmem_limit_bytes=48 * 2**20),
-    )(wide, conv_in.reshape(864, 32), conv_out.reshape(864, 32), norm_gain.reshape(1, 256), q_weight, kv_weight, out_weight, up_weight)
+    )(*(pltpu.with_memory_space_constraint(a, pltpu.HBM) for a in (volume, conv_in.reshape(864, 32), conv_out.reshape(864, 32), norm_gain.reshape(1, 256), q_weight, kv_weight, out_weight, up_weight)))
     return result.reshape(8, 32, 16, 32)
 
 

time: 55.6 us -> 52 us (0.935)
  local copies, waits for them, and re-layouts: 3.89 us -> 1.56 us
  Pallas kernels: 51.4 us -> 50.3 us
    reshape x1 -> x0, local copies, waits for them, and re-layouts: 2.3 us -> none  [on_device(): wide = volume.reshape(8, 32, 512)]
    pallas_call x1, Pallas kernels: 51.4 us -> 50.3 us  [on_device(): pl.pallas_call(functools.partial(kernel, sizes), out_shape=jax.ShapeDtype...]
where the time goes in v2:
time: 52 us; the launch traced here: 51.8 us
  Pallas kernels  50.3 us (97%)
  local copies, waits for them, and re-layouts  1.56 us (3%)
    pallas_call x1, Pallas kernels, on_device(): pl.pallas_call(functools.partial(kernel, sizes), out_shape=jax.ShapeDtype...  50.3 us
    reshape x1, local copies, waits for them, and re-layouts, on_device(): return result.reshape(8, 32, 16, 32)  1.56 us

profile of v2, /device:TPU:1, one launch (start us, length us, event | category | flops | bytes accessed | tf_op | source)
XLA Modules:
  0.0 51.8 jit_solution(6908330401629807153)
XLA Ops:
  0.0 50.3 %shard_map.82 = bf16[8,32,512]{2,1,0:T(8,128)(2,1)S(1)} custom-call(bf16[8,32,16,32]{3,2,1,0:T(8,128)(2,1)} %x_hbm.1, bf16[864,32]{1,0:T(8,128)(2,1)} %bitcast.3, bf16[864,32]{1,0:T(8,128)(2,1)} %bitcast.4, f32[1,256]{1,0:T(1,128)} %bitcast.5, bf16[256,256]{1,0:T(8,128)(2,1)} %qw_hbm.1, bf16[256,512]{1,0:T(8,128)(2,1)} %kvw_hbm.1, bf16[256,256]{1,0:T(8,128)(2,1)} %ow_hbm.1, ...), custom_call_target="tpu_custom_call" | custom-call | tf_op jit(solution)/shard_map/pallas_call | solution.py:386
  50.3 1.6 %reshape.15 = bf16[8,32,16,32]{3,2,1,0:T(8,128)(2,1)} reshape(bf16[8,32,512]{2,1,0:T(8,128)(2,1)S(1)} %shard_map.82) | data formatting | bytes 524288 | tf_op jit(solution)/shard_map/reshape | solution.py:394

commit v3 on v2

--- a/solution.py
+++ b/solution.py
@@ -46,11 +46,16 @@
     def at_mesh(x, y, z):
         return (x, y, z)
 
+    row_y = [(gy + 2 * k) % GY for k in range(GY // 2)]
+    row_z = [(gz + k) % GZ for k in range(GZ)]
+    col_x = [(gx + k) % GX for k in range(GX)]
+    col_y = [gy, gy // 2 * 2 + (gy + 1) % 2]
+
     def row_peer(i, sign=1):
-        return at_mesh(gx, (gy + GY + sign * 2 * (i // GZ)) % GY, (gz + GZ + sign * (i % GZ)) % GZ)
+        return at_mesh(gx, row_y[sign * (i // GZ) % (GY // 2)], row_z[sign * (i % GZ) % GZ])
 
     def col_peer(i):
-        return at_mesh((gx + i // 2) % GX, gy // 2 * 2 + (gy + i % 2) % 2, gz)
+        return at_mesh(col_x[i // 2], col_y[i % 2], gz)
 
     row_far = sorted(range(1, n_row), key=lambda i: -2 * min(i // GZ, GY // 2 - i // GZ) - min(i % GZ // 2, GZ // 2 - i % GZ // 2) - i % 2)
     col_far = sorted(range(1, n_col), key=lambda i: -min(i // 2, GX - i // 2))
@@ -143,15 +148,19 @@
             for dy in range(3):
                 first = (dx * 3 + dy) * 96
                 for m in range(2):
-                    for block in range(6):
+                    for z in range(8):
                         total = None
                         for g in range(4):
-                            dz = block - g
+                            dz = z - 4 * m - g + 1
                             if 0 <= dz <= 2:
                                 piece = moved[first + dz * 32:first + dz * 32 + 32, g * 128:g * 128 + 128]
                                 total = piece if total is None else total + piece
-                        r0 = dx * 512 + (4 * m + 3 + block) * 32
-                        taps[dy, r0:r0 + 32, m * 128:m * 128 + 128] = total
+                        if total is not None:
+                            r0 = dx * 256 + z * 32
+                            taps[dy, r0:r0 + 32, m * 128:m * 128 + 128] = total
+                above, below = 768 + 32 * (0, 2, 4)[dx], 768 + 32 * (3, 1, 7)[dx]
+                taps[dy, above:above + 32, 128:256] = moved[first + 64:first + 96, 384:512]
+                taps[dy, below:below + 32, 0:128] = moved[first:first + 32, 0:128]
 
     def convolve(main, lo, hi, emit):
         row8 = iota((8, 768), 0)
@@ -161,11 +170,22 @@
             return (jnp.where(row8 == 0, roll(before, 1, 0), roll(here, 1, 0)), here,
                     jnp.where(row8 == 7, roll(after, 7, 0), roll(here, 7, 0)))
 
-        rims = [jnp.concatenate(p, axis=0).astype(BF) for p in zip(three(lo), three(hi))]
-        for dx in range(3):
-            for h in range(2):
-                lhs[h * 256:h * 256 + 256, dx * 512:dx * 512 + 512] = main[dx:dx + 8, :, h * 256:h * 256 + 512].reshape(256, 512)
-                lhs[512 + 16 * h:528 + 16 * h, dx * 512:dx * 512 + 512] = rims[dx][:, h * 256:h * 256 + 512]
+        rims = [jnp.concatenate(p, axis=0) for p in zip(three(lo), three(hi))]
+        g = iota((1, 128), 1) // 32
+        last, first = (g == 3).astype(F32), (g == 0).astype(F32)
+        for h, (a, b) in enumerate(((0, 384), (256, 640))):
+            rows, few = slice(h * 256, h * 256 + 256), slice(512 + 16 * h, 528 + 16 * h)
+            o = 128 + 256 * h
+            for dx in range(3):
+                lhs[rows, dx * 256:dx * 256 + 256] = main[dx:dx + 8, :, o:o + 256].reshape(256, 256)
+                lhs[few, dx * 256:dx * 256 + 256] = rims[dx][:, o:o + 256].astype(BF)
+            ends = (main[:, :, a:a + 128].reshape(320, 128) * last.astype(BF) + main[:, :, b:b + 128].reshape(320, 128) * first.astype(BF))
+            turned = roll(ends[32:288].astype(F32), 64, 1).astype(BF)
+            lhs[rows, 768:896] = ends[0:256] + turned
+            lhs[rows, 896:1024] = ends[64:320]
+            ends = [rim[:, a:a + 128] * last + rim[:, b:b + 128] * first for rim in rims]
+            lhs[few, 768:896] = (ends[0] + roll(ends[1], 64, 1)).astype(BF)
+            lhs[few, 896:1024] = ends[2].astype(BF)
 
         def one(dy, carry):
             acc[dy, 0:544, :] = dot(lhs[...], taps[dy])
@@ -238,12 +258,11 @@
     kv_all = pltpu.make_async_copy(kvbuf.at[pl.ds(1, n_col - 1)], kvbuf.at[pl.ds(1, n_col - 1)], gr.at[1])
     q_gone = pltpu.make_async_copy(qbuf.at[pl.ds(1, n_row - 1)], qbuf.at[pl.ds(1, n_row - 1)], gs.at[0])
     kv_gone = pltpu.make_async_copy(kvbuf.at[pl.ds(1, n_col - 1)], kvbuf.at[pl.ds(1, n_col - 1)], gs.at[1])
-    for i in row_far:
-        pltpu.make_async_remote_copy(src_ref=qbuf.at[0], dst_ref=qbuf.at[i], send_sem=gs.at[0], recv_sem=gr.at[0],
-                                     device_id=row_peer(i), device_id_type=MESH).start()
-    for i in col_far:
-        pltpu.make_async_remote_copy(src_ref=kvbuf.at[0], dst_ref=kvbuf.at[i], send_sem=gs.at[1], recv_sem=gr.at[1],
-                                     device_id=col_peer(i), device_id_type=MESH).start()
+    sends = [(n / len(row_far), qbuf, 0, i, row_peer(i)) for n, i in enumerate(row_far)]
+    sends += [(n / len(col_far), kvbuf, 1, i, col_peer(i)) for n, i in enumerate(col_far)]
+    for _, buf, n, i, peer in sorted(sends, key=lambda s: s[0]):
+        pltpu.make_async_remote_copy(src_ref=buf.at[0], dst_ref=buf.at[i], send_sem=gs.at[n], recv_sem=gr.at[n],
+                                     device_id=peer, device_id_type=MESH).start()
     pack_rows(enc, rows_e)
     enc_copies = halo_copies(enc, rows_e, enc_lo, enc_hi, es, er)
     start_all(enc_copies)
@@ -329,6 +348,13 @@
         dy = {-1: pl.ds(9, 1), 0: pl.ds(1, 8), 1: pl.ds(0, 1)}[b]
         up_copies.append(remote(up.at[sx, sy, pl.ds(0, 1)], uppad.at[dx, dy, pl.ds(1 - c, 1)], us.at[n], ur.at[n], (a, b, c)))
     start_all(up_copies)
+    departed(vol_copies)
+    departed(enc_copies)
+    departed(up_copies)
+    q_gone.wait()
+    kv_gone.wait()
+    pltpu.make_async_copy(orecv.at[others], orecv.at[others], rs.at[0]).wait()
+    pltpu.make_async_copy(lrecv.at[others], lrecv.at[others], rs.at[1]).wait()
     arrived(up_copies)
 
     group1 = iota((1, 128), 1) // 32
@@ -362,14 +388,6 @@
 
     convolve(joi, joi_lo, joi_hi, keep_result)
 
-    departed(vol_copies)
-    departed(enc_copies)
-    departed(up_copies)
-    q_gone.wait()
-    kv_gone.wait()
-    pltpu.make_async_copy(orecv.at[others], orecv.at[others], rs.at[0]).wait()
-    pltpu.make_async_copy(lrecv.at[others], lrecv.at[others], rs.at[1]).wait()
-
 
 def on_device(sizes, volume, conv_in, conv_out, norm_gain, q_weight, kv_weight, out_weight, up_weight):
     n_row, n_col = (sizes[1] // 2) * sizes[2], sizes[0] * 2
@@ -377,7 +395,7 @@
     vmem = pltpu.VMEM
     scratch = [vmem((8, 32, 16, 32), BF)] + [vmem(padded, BF), vmem(rim, BF), vmem(rim, BF)] * 3 + [vmem(rows, BF)] * 2
     scratch += [vmem((864, 32), BF)] * 2 + [vmem((1, 256), F32), vmem((256, 256), BF), vmem((256, 512), BF), vmem((256, 256), BF), vmem((256, 256), BF)]
-    scratch += [vmem((3, 1536, 256), BF), vmem((544, 1536), BF), vmem((3, 552, 256), F32), vmem((8, 256), F32)]
+    scratch += [vmem((3, 1024, 256), BF), vmem((544, 1024), BF), vmem((3, 552, 256), F32), vmem((8, 256), F32)]
     scratch += [vmem((n_row, 16, 128), BF), vmem((n_col, 32, 128), BF), vmem((4, n_col * 16, 128), BF), vmem((4, n_col * 16, 256), BF)]
     scratch += [vmem((n_row, 16, 128), BF)] * 2 + [vmem((n_row, 1, 128), F32)] * 2
     scratch += [vmem((2, 8, 1, 1, 128), F32), vmem((4, 10, 3, 1, 128), F32)]

time: 52 us -> 51.3 us (0.987)
  Pallas kernels: 50.3 us -> 49.6 us
    pallas_call x1, Pallas kernels: 50.3 us -> 49.6 us  [on_device(): pl.pallas_call(functools.partial(kernel, sizes), out_shape=jax.ShapeDtype...]
where the time goes in v3:
time: 51.3 us; the launch traced here: 51.2 us
  Pallas kernels  49.6 us (97%)
  local copies, waits for them, and re-layouts  1.56 us (3%)
    pallas_call x1, Pallas kernels, on_device(): pl.pallas_call(functools.partial(kernel, sizes), out_shape=jax.ShapeDtype...  49.6 us
    reshape x1, local copies, waits for them, and re-layouts, on_device(): return result.reshape(8, 32, 16, 32)  1.56 us

profile of v3, /device:TPU:1, one launch (start us, length us, event | category | flops | bytes accessed | tf_op | source)
XLA Modules:
  0.0 51.2 jit_solution(10880010642394588543)
XLA Ops:
  0.0 49.6 %shard_map.82 = bf16[8,32,512]{2,1,0:T(8,128)(2,1)S(1)} custom-call(bf16[8,32,16,32]{3,2,1,0:T(8,128)(2,1)} %x_hbm.1, bf16[864,32]{1,0:T(8,128)(2,1)} %bitcast.3, bf16[864,32]{1,0:T(8,128)(2,1)} %bitcast.4, f32[1,256]{1,0:T(1,128)} %bitcast.5, bf16[256,256]{1,0:T(8,128)(2,1)} %qw_hbm.1, bf16[256,512]{1,0:T(8,128)(2,1)} %kvw_hbm.1, bf16[256,256]{1,0:T(8,128)(2,1)} %ow_hbm.1, ...), custom_call_target="tpu_custom_call" | custom-call | tf_op jit(solution)/shard_map/pallas_call | solution.py:404
  49.6 1.6 %reshape.15 = bf16[8,32,16,32]{3,2,1,0:T(8,128)(2,1)} reshape(bf16[8,32,512]{2,1,0:T(8,128)(2,1)S(1)} %shard_map.82) | data formatting | bytes 524288 | tf_op jit(solution)/shard_map/reshape | solution.py:412

commit v4 on v3

--- a/solution.py
+++ b/solution.py
@@ -79,14 +79,14 @@
     for ref in (vol_lo, vol_hi, enc_lo, enc_hi, uppad):
         ref[...] = jnp.zeros(ref.shape, ref.dtype)
     barrier = pltpu.get_barrier_semaphore()
+    for i in row_far:
+        pl.semaphore_signal(barrier, inc=1, device_id=row_peer(i), device_id_type=MESH)
+    for i in col_far:
+        pl.semaphore_signal(barrier, inc=1, device_id=col_peer(i), device_id_type=MESH)
     for step in STEPS:
         @pl.when(inside(*step))
         def _(step=step):
             pl.semaphore_signal(barrier, inc=1, device_id=neighbour(*step), device_id_type=MESH)
-    for i in range(1, n_row):
-        pl.semaphore_signal(barrier, inc=1, device_id=row_peer(i), device_id_type=MESH)
-    for i in range(1, n_col):
-        pl.semaphore_signal(barrier, inc=1, device_id=col_peer(i), device_id_type=MESH)
 
     own = (pl.ds(1, 8), pl.ds(0, 32), pl.ds(128, 512))
     loads = [pltpu.make_async_copy(x_hbm, raw, load_sem.at[0])]
@@ -162,6 +162,13 @@
                 taps[dy, above:above + 32, 128:256] = moved[first + 64:first + 96, 384:512]
                 taps[dy, below:below + 32, 0:128] = moved[first:first + 32, 0:128]
 
+    def lay_own(main):
+        for h in range(2):
+            o = 128 + 256 * h
+            for dx, x0, x1 in ((0, 1, 8), (1, 0, 8), (2, 0, 7)):
+                planes = main[x0 + dx:x1 + dx, :, o:o + 256].reshape((x1 - x0) * 32, 256)
+                lhs[h * 256 + 32 * x0:h * 256 + 32 * x1, dx * 256:dx * 256 + 256] = planes
+
     def convolve(main, lo, hi, emit):
         row8 = iota((8, 768), 0)
 
@@ -177,7 +184,9 @@
             rows, few = slice(h * 256, h * 256 + 256), slice(512 + 16 * h, 528 + 16 * h)
             o = 128 + 256 * h
             for dx in range(3):
-                lhs[rows, dx * 256:dx * 256 + 256] = main[dx:dx + 8, :, o:o + 256].reshape(256, 256)
+                if dx != 1:
+                    edge, plane = (h * 256, 0) if dx == 0 else (h * 256 + 224, 9)
+                    lhs[edge:edge + 32, dx * 256:dx * 256 + 256] = main[plane, :, o:o + 256]
                 lhs[few, dx * 256:dx * 256 + 256] = rims[dx][:, o:o + 256].astype(BF)
             ends = (main[:, :, a:a + 128].reshape(320, 128) * last.astype(BF) + main[:, :, b:b + 128].reshape(320, 128) * first.astype(BF))
             turned = roll(ends[32:288].astype(F32), 64, 1).astype(BF)
@@ -216,6 +225,7 @@
     start_all(vol_copies)
     for copy in loads[1:]:
         copy.wait()
+    lay_own(vol)
     spread_taps(win)
     arrived(vol_copies)
 
@@ -285,8 +295,8 @@
     group = iota((n_rows, 128), 1) // 32
     compact = iota((slots, 16, 128), 1) == iota((slots, 16, 128), 2) % 32
 
-    def attend(i, carry):
-        at = pl.ds(i * slots, slots)
+    def attend(i):
+        at = slice(i * slots, i * slots + slots)
         query = qbuf[at].reshape(n_rows, 128)
         total, peaks = jnp.zeros((n_rows, 256), F32), jnp.zeros((n_rows, 128), F32)
         for g in range(4):
@@ -299,15 +309,15 @@
         osend[at] = (total[:, 0:128] / weight).astype(BF).reshape(slots, 16, 128)
         level = (peaks + jnp.log(weight)).reshape(slots, 16, 128)
         lsend[at] = jnp.sum(jnp.where(compact, level, 0.0), axis=1, keepdims=True)
-        return carry
-
-    lax.fori_loop(0, n_row // slots, attend, 0)
+
     others = pl.ds(1, n_row - 1)
-    for i in row_far:
-        pltpu.make_async_remote_copy(src_ref=lsend.at[i], dst_ref=lrecv.at[i], send_sem=rs.at[1], recv_sem=rr.at[1],
-                                     device_id=row_peer(i, -1), device_id_type=MESH).start()
-        pltpu.make_async_remote_copy(src_ref=osend.at[i], dst_ref=orecv.at[i], send_sem=rs.at[0], recv_sem=rr.at[0],
-                                     device_id=row_peer(i, -1), device_id_type=MESH).start()
+    n_blocks = n_row // slots
+    for block in sorted(range(n_blocks), key=lambda k: -min(k, n_blocks - k)):
+        attend(block)
+        for i in [i for i in row_far if i // slots == block]:
+            for n, (src, dst) in enumerate(((osend, orecv), (lsend, lrecv))):
+                pltpu.make_async_remote_copy(src_ref=src.at[i], dst_ref=dst.at[i], send_sem=rs.at[n], recv_sem=rr.at[n],
+                                             device_id=row_peer(i, -1), device_id_type=MESH).start()
     orecv[0] = osend[0]
     lrecv[0] = lsend[0]
     arrived(enc_copies)
@@ -355,27 +365,41 @@
     kv_gone.wait()
     pltpu.make_async_copy(orecv.at[others], orecv.at[others], rs.at[0]).wait()
     pltpu.make_async_copy(lrecv.at[others], lrecv.at[others], rs.at[1]).wait()
-    arrived(up_copies)
 
     group1 = iota((1, 128), 1) // 32
 
-    def wide(plane, y):
-        middle = uppad[plane, y, 1]
-        parts = [uppad[plane, y, 0]]
+    def middle(plane, y):
+        here = uppad[plane, y, 1]
+        parts = []
         for q in range(4):
-            part = jnp.where(group1 == q, middle, 0.0)
+            part = jnp.where(group1 == q, here, 0.0)
             part = part + roll(part, 64, 1)
             parts.append(part + roll(part, 32, 1))
-        return jnp.concatenate(parts + [uppad[plane, y, 2]], axis=1)
-
-    row_wide = iota((8, 768), 0)
-    for plane in range(4):
-        xs = (range(0, 1), range(1, 5), range(5, 9), range(9, 10))[plane]
-        for y2 in range(2):
-            four = [wide(plane, 1 + 4 * y2 + i) for i in range(4)]
-            more = jnp.concatenate([jnp.where(row_wide < 4, four[2 * i], four[2 * i + 1]) for i in range(2)], axis=0)
-            for x in xs:
-                joi[x, 16 * y2:16 * y2 + 16, :] = (enc[x, 16 * y2:16 * y2 + 16, :].astype(F32) + more).astype(BF)
+        return jnp.concatenate(parts, axis=1)
+
+    def wide(plane, y):
+        return jnp.concatenate([uppad[plane, y, 0], middle(plane, y), uppad[plane, y, 2]], axis=1)
+
+    def side(n):
+        return lambda plane, y: uppad[plane, y, n]
+
+    def join_planes(planes, first, width, row_of):
+        row = iota((8, width), 0)
+        for plane in planes:
+            xs = (range(0, 1), range(1, 5), range(5, 9), range(9, 10))[plane]
+            for y2 in range(2):
+                four = [row_of(plane, 1 + 4 * y2 + i) for i in range(4)]
+                more = jnp.concatenate([jnp.where(row < 4, four[2 * i], four[2 * i + 1]) for i in range(2)], axis=0)
+                for x in xs:
+                    here = (x, slice(16 * y2, 16 * y2 + 16), slice(first, first + width))
+                    joi[here] = (enc[here].astype(F32) + more).astype(BF)
+
+    join_planes((1, 2), 128, 512, middle)
+    lay_own(joi)
+    arrived(up_copies)
+    join_planes((1, 2), 0, 128, side(0))
+    join_planes((1, 2), 640, 128, side(2))
+    join_planes((0, 3), 0, 768, wide)
     row_rim = iota((16, 768), 0)
     for rim, full, y in ((enc_lo, joi_lo, 0), (enc_hi, joi_hi, 9)):
         planes = [wide(plane, y) for plane in range(4)]

time: 51.3 us -> 50.1 us (0.977)
  Pallas kernels: 49.6 us -> 48 us
    pallas_call x1, Pallas kernels: 49.6 us -> 48 us  [on_device(): pl.pallas_call(functools.partial(kernel, sizes), out_shape=jax.ShapeDtype...]
where the time goes in v4:
time: 50.1 us; the launch traced here: 49.6 us
  Pallas kernels  48 us (96%)
  local copies, waits for them, and re-layouts  1.56 us (3%)
    pallas_call x1, Pallas kernels, on_device(): pl.pallas_call(functools.partial(kernel, sizes), out_shape=jax.ShapeDtype...  48 us
    reshape x1, local copies, waits for them, and re-layouts, on_device(): return result.reshape(8, 32, 16, 32)  1.56 us

profile of v4, /device:TPU:1, one launch (start us, length us, event | category | flops | bytes accessed | tf_op | source)
XLA Modules:
  0.0 49.6 jit_solution(15494282909027650692)
XLA Ops:
  0.0 48.0 %shard_map.82 = bf16[8,32,512]{2,1,0:T(8,128)(2,1)S(1)} custom-call(bf16[8,32,16,32]{3,2,1,0:T(8,128)(2,1)} %x_hbm.1, bf16[864,32]{1,0:T(8,128)(2,1)} %bitcast.3, bf16[864,32]{1,0:T(8,128)(2,1)} %bitcast.4, f32[1,256]{1,0:T(1,128)} %bitcast.5, bf16[256,256]{1,0:T(8,128)(2,1)} %qw_hbm.1, bf16[256,512]{1,0:T(8,128)(2,1)} %kvw_hbm.1, bf16[256,256]{1,0:T(8,128)(2,1)} %ow_hbm.1, ...), custom_call_target="tpu_custom_call" | custom-call | tf_op jit(solution)/shard_map/pallas_call | solution.py:428
  48.1 1.6 %reshape.15 = bf16[8,32,16,32]{3,2,1,0:T(8,128)(2,1)} reshape(bf16[8,32,512]{2,1,0:T(8,128)(2,1)S(1)} %shard_map.82) | data formatting | bytes 524288 | tf_op jit(solution)/shard_map/reshape | solution.py:436

commit v5 on v4

--- a/solution.py
+++ b/solution.py
@@ -35,7 +35,7 @@
 
 
 def kernel(sizes, x_hbm, win_hbm, wout_hbm, gain_hbm, qw_hbm, kvw_hbm, ow_hbm, uw_hbm, out_ref,
-           raw, vol, vol_lo, vol_hi, enc, enc_lo, enc_hi, joi, joi_lo, joi_hi, rows_v, rows_e,
+           raw, vol, vol_lo, vol_hi, enc, enc_lo, enc_hi, joi, joi_lo, joi_hi, rows_v, rows_e, ends_s, ends_r,
            win, wout, gain, qw, kvw, ow, uw, taps, lhs, acc, tokens_s,
            qbuf, kvbuf, kmask, vmask, osend, orecv, lsend, lrecv, up, uppad,
            load_sem, vs, vr, es, er, us, ur, gs, gr, rs, rr):
@@ -74,9 +74,9 @@
     for ref in (vol, enc):
         for x in (0, 9):
             ref[x] = jnp.zeros((32, 768), BF)
-        for z in (0, 640):
-            ref[1:9, :, z:z + 128] = jnp.zeros((8, 32, 128), BF)
-    for ref in (vol_lo, vol_hi, enc_lo, enc_hi, uppad):
+    for z in (0, 640):
+        enc[1:9, :, z:z + 128] = jnp.zeros((8, 32, 128), BF)
+    for ref in (ends_r, vol_lo, vol_hi, enc_lo, enc_hi, uppad):
         ref[...] = jnp.zeros(ref.shape, ref.dtype)
     barrier = pltpu.get_barrier_semaphore()
     for i in row_far:
@@ -106,11 +106,30 @@
                                             device_id=neighbour(*step), device_id_type=MESH)
         return copy, pltpu.make_async_copy(dst, dst, recv), pltpu.make_async_copy(src, src, send)
 
-    def halo_copies(main, rows, lo, hi, send, recv):
+    def turn(value, groups):
+        return roll(value, 32 * groups % 128, 1) if groups % 4 else value
+
+    def pack_ends(main):
+        group = iota((32, 128), 1) // 32
+        for n, (first, at) in enumerate(((128, 0), (512, 3))):
+            for p in range(2):
+                planes = [jnp.where(group == at, main[1 + 2 * g + p, :, first:first + 128].astype(F32), 0.0) for g in range(4)]
+                ends_s[n, p] = sum(turn(v, g - at) for g, v in enumerate(planes)).astype(BF)
+
+    def unpack_ends(main):
+        for n, (first, at) in enumerate(((640, 0), (0, 3))):
+            for p in range(2):
+                value = ends_r[n, p].astype(F32)
+                for g in range(4):
+                    main[1 + 2 * g + p, :, first:first + 128] = turn(value, at - g).astype(BF)
+
+    def halo_copies(main, rows, lo, hi, send, recv, packed=False):
         copies = []
         for n, (a, b, c) in enumerate(STEPS):
             (s0, width), (d0, _) = lane_window(c, 512)
-            if b == 0:
+            if packed and a == 0 and b == 0:
+                src, dst = ends_s.at[(c + 1) // 2], ends_r.at[(c + 1) // 2]
+            elif b == 0:
                 sx = {-1: pl.ds(1, 1), 0: pl.ds(1, 8), 1: pl.ds(8, 1)}[a]
                 dx = {-1: pl.ds(9, 1), 0: pl.ds(1, 8), 1: pl.ds(0, 1)}[a]
                 src = main.at[sx, pl.ds(0, 32), pl.ds(128 + s0, width)]
@@ -217,17 +236,19 @@
     for x in range(8):
         vol[1 + x, :, 128:640] = raw[x].reshape(32, 512)
     pack_rows(vol, rows_v)
+    pack_ends(vol)
     neighbours = (1 + (gx > 0).astype(jnp.int32) + (gx < GX - 1).astype(jnp.int32))
     neighbours *= (1 + (gy > 0).astype(jnp.int32) + (gy < GY - 1).astype(jnp.int32))
     neighbours *= (1 + (gz > 0).astype(jnp.int32) + (gz < GZ - 1).astype(jnp.int32))
     pl.semaphore_wait(barrier, neighbours - 1 + n_row - 1 + n_col - 1)
-    vol_copies = halo_copies(vol, rows_v, vol_lo, vol_hi, vs, vr)
+    vol_copies = halo_copies(vol, rows_v, vol_lo, vol_hi, vs, vr, True)
     start_all(vol_copies)
     for copy in loads[1:]:
         copy.wait()
     lay_own(vol)
     spread_taps(win)
     arrived(vol_copies)
+    unpack_ends(vol)
 
     def keep_encoded(x, h, value):
         enc[1 + x, :, 128 + 256 * h:384 + 256 * h] = jnp.maximum(value, 0.0).astype(BF)
@@ -417,7 +438,7 @@
     n_row, n_col = (sizes[1] // 2) * sizes[2], sizes[0] * 2
     padded, rim, rows = (10, 32, 768), (3, 16, 768), (2, 16, 512)
     vmem = pltpu.VMEM
-    scratch = [vmem((8, 32, 16, 32), BF)] + [vmem(padded, BF), vmem(rim, BF), vmem(rim, BF)] * 3 + [vmem(rows, BF)] * 2
+    scratch = [vmem((8, 32, 16, 32), BF)] + [vmem(padded, BF), vmem(rim, BF), vmem(rim, BF)] * 3 + [vmem(rows, BF)] * 2 + [vmem((2, 2, 32, 128), BF)] * 2
     scratch += [vmem((864, 32), BF)] * 2 + [vmem((1, 256), F32), vmem((256, 256), BF), vmem((256, 512), BF), vmem((256, 256), BF), vmem((256, 256), BF)]
     scratch += [vmem((3, 1024, 256), BF), vmem((544, 1024), BF), vmem((3, 552, 256), F32), vmem((8, 256), F32)]
     scratch += [vmem((n_row, 16, 128), BF), vmem((n_col, 32, 128), BF), vmem((4, n_col * 16, 128), BF), vmem((4, n_col * 16, 256), BF)]

time: 50.1 us -> 48.5 us (0.968)
  Pallas kernels: 48 us -> 46.7 us
    pallas_call x1, Pallas kernels: 48 us -> 46.7 us  [on_device(): pl.pallas_call(functools.partial(kernel, sizes), out_shape=jax.ShapeDtype...]
where the time goes in v5:
time: 48.5 us; the launch traced here: 48.2 us
  Pallas kernels  46.7 us (96%)
  local copies, waits for them, and re-layouts  1.56 us (3%)
    pallas_call x1, Pallas kernels, on_device(): pl.pallas_call(functools.partial(kernel, sizes), out_shape=jax.ShapeDtype...  46.7 us
    reshape x1, local copies, waits for them, and re-layouts, on_device(): return result.reshape(8, 32, 16, 32)  1.56 us

profile of v5, /device:TPU:1, one launch (start us, length us, event | category | flops | bytes accessed | tf_op | source)
XLA Modules:
  0.0 48.2 jit_solution(4092632070644522722)
XLA Ops:
  0.0 46.7 %shard_map.82 = bf16[8,32,512]{2,1,0:T(8,128)(2,1)S(1)} custom-call(bf16[8,32,16,32]{3,2,1,0:T(8,128)(2,1)} %x_hbm.1, bf16[864,32]{1,0:T(8,128)(2,1)} %bitcast.3, bf16[864,32]{1,0:T(8,128)(2,1)} %bitcast.4, f32[1,256]{1,0:T(1,128)} %bitcast.5, bf16[256,256]{1,0:T(8,128)(2,1)} %qw_hbm.1, bf16[256,512]{1,0:T(8,128)(2,1)} %kvw_hbm.1, bf16[256,256]{1,0:T(8,128)(2,1)} %ow_hbm.1, ...), custom_call_target="tpu_custom_call" | custom-call | tf_op jit(solution)/shard_map/pallas_call | solution.py:449
  46.7 1.6 %reshape.15 = bf16[8,32,16,32]{3,2,1,0:T(8,128)(2,1)} reshape(bf16[8,32,512]{2,1,0:T(8,128)(2,1)S(1)} %shard_map.82) | data formatting | bytes 524288 | tf_op jit(solution)/shard_map/reshape | solution.py:457

commit v6 on v5

--- a/solution.py
+++ b/solution.py
@@ -35,7 +35,7 @@
 
 
 def kernel(sizes, x_hbm, win_hbm, wout_hbm, gain_hbm, qw_hbm, kvw_hbm, ow_hbm, uw_hbm, out_ref,
-           raw, vol, vol_lo, vol_hi, enc, enc_lo, enc_hi, joi, joi_lo, joi_hi, rows_v, rows_e, ends_s, ends_r,
+           raw, vol, vol_lo, vol_hi, enc, enc_lo, enc_hi, joi, joi_lo, joi_hi, rows_v, rows_e, ends_s, ends_r, enc_s, enc_r,
            win, wout, gain, qw, kvw, ow, uw, taps, lhs, acc, tokens_s,
            qbuf, kvbuf, kmask, vmask, osend, orecv, lsend, lrecv, up, uppad,
            load_sem, vs, vr, es, er, us, ur, gs, gr, rs, rr):
@@ -74,9 +74,7 @@
     for ref in (vol, enc):
         for x in (0, 9):
             ref[x] = jnp.zeros((32, 768), BF)
-    for z in (0, 640):
-        enc[1:9, :, z:z + 128] = jnp.zeros((8, 32, 128), BF)
-    for ref in (ends_r, vol_lo, vol_hi, enc_lo, enc_hi, uppad):
+    for ref in (ends_r, enc_r, vol_lo, vol_hi, enc_lo, enc_hi, uppad):
         ref[...] = jnp.zeros(ref.shape, ref.dtype)
     barrier = pltpu.get_barrier_semaphore()
     for i in row_far:
@@ -109,26 +107,26 @@
     def turn(value, groups):
         return roll(value, 32 * groups % 128, 1) if groups % 4 else value
 
-    def pack_ends(main):
+    def pack_ends(main, out):
         group = iota((32, 128), 1) // 32
         for n, (first, at) in enumerate(((128, 0), (512, 3))):
             for p in range(2):
                 planes = [jnp.where(group == at, main[1 + 2 * g + p, :, first:first + 128].astype(F32), 0.0) for g in range(4)]
-                ends_s[n, p] = sum(turn(v, g - at) for g, v in enumerate(planes)).astype(BF)
-
-    def unpack_ends(main):
+                out[n, p] = sum(turn(v, g - at) for g, v in enumerate(planes)).astype(BF)
+
+    def unpack_ends(main, into):
         for n, (first, at) in enumerate(((640, 0), (0, 3))):
             for p in range(2):
-                value = ends_r[n, p].astype(F32)
+                value = into[n, p].astype(F32)
                 for g in range(4):
                     main[1 + 2 * g + p, :, first:first + 128] = turn(value, at - g).astype(BF)
 
-    def halo_copies(main, rows, lo, hi, send, recv, packed=False):
+    def halo_copies(main, rows, lo, hi, send, recv, out, into):
         copies = []
         for n, (a, b, c) in enumerate(STEPS):
             (s0, width), (d0, _) = lane_window(c, 512)
-            if packed and a == 0 and b == 0:
-                src, dst = ends_s.at[(c + 1) // 2], ends_r.at[(c + 1) // 2]
+            if a == 0 and b == 0:
+                src, dst = out.at[(c + 1) // 2], into.at[(c + 1) // 2]
             elif b == 0:
                 sx = {-1: pl.ds(1, 1), 0: pl.ds(1, 8), 1: pl.ds(8, 1)}[a]
                 dx = {-1: pl.ds(9, 1), 0: pl.ds(1, 8), 1: pl.ds(0, 1)}[a]
@@ -236,19 +234,19 @@
     for x in range(8):
         vol[1 + x, :, 128:640] = raw[x].reshape(32, 512)
     pack_rows(vol, rows_v)
-    pack_ends(vol)
+    pack_ends(vol, ends_s)
     neighbours = (1 + (gx > 0).astype(jnp.int32) + (gx < GX - 1).astype(jnp.int32))
     neighbours *= (1 + (gy > 0).astype(jnp.int32) + (gy < GY - 1).astype(jnp.int32))
     neighbours *= (1 + (gz > 0).astype(jnp.int32) + (gz < GZ - 1).astype(jnp.int32))
     pl.semaphore_wait(barrier, neighbours - 1 + n_row - 1 + n_col - 1)
-    vol_copies = halo_copies(vol, rows_v, vol_lo, vol_hi, vs, vr, True)
+    vol_copies = halo_copies(vol, rows_v, vol_lo, vol_hi, vs, vr, ends_s, ends_r)
     start_all(vol_copies)
     for copy in loads[1:]:
         copy.wait()
     lay_own(vol)
     spread_taps(win)
     arrived(vol_copies)
-    unpack_ends(vol)
+    unpack_ends(vol, ends_r)
 
     def keep_encoded(x, h, value):
         enc[1 + x, :, 128 + 256 * h:384 + 256 * h] = jnp.maximum(value, 0.0).astype(BF)
@@ -295,7 +293,8 @@
         pltpu.make_async_remote_copy(src_ref=buf.at[0], dst_ref=buf.at[i], send_sem=gs.at[n], recv_sem=gr.at[n],
                                      device_id=peer, device_id_type=MESH).start()
     pack_rows(enc, rows_e)
-    enc_copies = halo_copies(enc, rows_e, enc_lo, enc_hi, es, er)
+    pack_ends(enc, enc_s)
+    enc_copies = halo_copies(enc, rows_e, enc_lo, enc_hi, es, er, enc_s, enc_r)
     start_all(enc_copies)
     spread_taps(wout)
 
@@ -342,6 +341,7 @@
     orecv[0] = osend[0]
     lrecv[0] = lsend[0]
     arrived(enc_copies)
+    unpack_ends(enc, enc_r)
     pltpu.make_async_copy(orecv.at[others], orecv.at[others], rr.at[0]).wait()
     pltpu.make_async_copy(lrecv.at[others], lrecv.at[others], rr.at[1]).wait()
 
@@ -438,7 +438,7 @@
     n_row, n_col = (sizes[1] // 2) * sizes[2], sizes[0] * 2
     padded, rim, rows = (10, 32, 768), (3, 16, 768), (2, 16, 512)
     vmem = pltpu.VMEM
-    scratch = [vmem((8, 32, 16, 32), BF)] + [vmem(padded, BF), vmem(rim, BF), vmem(rim, BF)] * 3 + [vmem(rows, BF)] * 2 + [vmem((2, 2, 32, 128), BF)] * 2
+    scratch = [vmem((8, 32, 16, 32), BF)] + [vmem(padded, BF), vmem(rim, BF), vmem(rim, BF)] * 3 + [vmem(rows, BF)] * 2 + [vmem((2, 2, 32, 128), BF)] * 4
     scratch += [vmem((864, 32), BF)] * 2 + [vmem((1, 256), F32), vmem((256, 256), BF), vmem((256, 512), BF), vmem((256, 256), BF), vmem((256, 256), BF)]
     scratch += [vmem((3, 1024, 256), BF), vmem((544, 1024), BF), vmem((3, 552, 256), F32), vmem((8, 256), F32)]
     scratch += [vmem((n_row, 16, 128), BF), vmem((n_col, 32, 128), BF), vmem((4, n_col * 16, 128), BF), vmem((4, n_col * 16, 256), BF)]

time: 48.5 us -> 48.3 us (level)
  no operation moved by 1% of the time
where the time goes in v6:
time: 48.3 us; the launch traced here: 48.1 us
  Pallas kernels  46.6 us (96%)
  local copies, waits for them, and re-layouts  1.56 us (3%)
    pallas_call x1, Pallas kernels, on_device(): pl.pallas_call(functools.partial(kernel, sizes), out_shape=jax.ShapeDtype...  46.6 us
    reshape x1, local copies, waits for them, and re-layouts, on_device(): return result.reshape(8, 32, 16, 32)  1.56 us

profile of v6, /device:TPU:1, one launch (start us, length us, event | category | flops | bytes accessed | tf_op | source)
XLA Modules:
  0.0 48.1 jit_solution(12286009334599012809)
XLA Ops:
  0.0 46.6 %shard_map.82 = bf16[8,32,512]{2,1,0:T(8,128)(2,1)S(1)} custom-call(bf16[8,32,16,32]{3,2,1,0:T(8,128)(2,1)} %x_hbm.1, bf16[864,32]{1,0:T(8,128)(2,1)} %bitcast.3, bf16[864,32]{1,0:T(8,128)(2,1)} %bitcast.4, f32[1,256]{1,0:T(1,128)} %bitcast.5, bf16[256,256]{1,0:T(8,128)(2,1)} %qw_hbm.1, bf16[256,512]{1,0:T(8,128)(2,1)} %kvw_hbm.1, bf16[256,256]{1,0:T(8,128)(2,1)} %ow_hbm.1, ...), custom_call_target="tpu_custom_call" | custom-call | tf_op jit(solution)/shard_map/pallas_call | solution.py:449
  46.6 1.6 %reshape.15 = bf16[8,32,16,32]{3,2,1,0:T(8,128)(2,1)} reshape(bf16[8,32,512]{2,1,0:T(8,128)(2,1)S(1)} %shard_map.82) | data formatting | bytes 524288 | tf_op jit(solution)/shard_map/reshape | solution.py:457
